TPU v7x, 256 devices: a whole 4x4x8 slice. The times are simulated.
256 devices in a mesh: cam: 8 (over x_hi, y), seq: 32 (over z, x_lo, core).
Axes of the slice: x: 4 (x_hi: 2, x_lo: 2; x = x_hi * 2 + x_lo), y: 4, z: 8, core: 2. Of those that a mesh axis runs over, the one named last changes fastest.
Arguments:
- q_tok: bfloat16 [8, 4096, 1536], P('cam', 'seq')
- k_tok: bfloat16 [8, 4096, 1536], P('cam', 'seq')
- v_tok: bfloat16 [8, 4096, 1536], P('cam', 'seq'), may hold values from -6 to 6
- strip_kv: bfloat16 [8, 2, 2, 1024, 1536], P('cam', None, None, 'seq')
- bev_keys: bfloat16 [32768, 1536], P(('cam', 'seq'))
- bev_values: bfloat16 [32768, 1536], P(('cam', 'seq')), may hold values from -6 to 6
- bev_list: int32 [8, 32, 3], P('cam', 'seq'), may hold values from 0 to 7, as said below
- bev_count: int32 [8, 32], P('cam', 'seq'), may hold values from 1 to 3, as said below
- gate_table: float32 [50, 3, 1536], replicated, may hold values from 0.1 to 1.9
- timestep: int32 [1], replicated, may hold values from 0 to 49
Outputs:
- blended: bfloat16 [8, 4096, 1536], P('cam', 'seq')
Inputs may be any that keep to these rules, and one draw needn't show every extreme that they name: The 3 entries of each row of bev_list are different cameras. `bev_count`: some token block uses all 3 entries.
All inputs are finite; a program needn't handle non-finite values.
Results may differ from a plain program's by a relative error of at most 0.0039.
Values may be sent and summed in bfloat16 or wider, within the bound.
No kernel may reach another device: no remote copies, remote signals or barrier semaphores. Data moves between devices by JAX's collectives and lax.ppermute only.
A program may use at most 128 MiB of HBM per device.

v0:
```python
import math

import jax
import jax.numpy as jnp
from jax import lax
from jax.sharding import PartitionSpec as P

HEADS = 24
LIST = 3


def from_behind(x, axis, by):
    peers = lax.axis_size(axis)
    return lax.ppermute(x, axis, [(i, (i + by) % peers) for i in range(peers)])


def online_step(state_in, queries, key_block, value_block, allowed):
    running_max, running_sum, accum_out = state_in
    head_size = queries.shape[2]
    scores = jnp.einsum("thd,rhd->htr", queries, key_block, preferred_element_type=jnp.float32) * (
        1.0 / math.sqrt(head_size)
    )
    if allowed is not None:
        scores = jnp.where(allowed, scores, -1e30)
    new_max = jnp.maximum(running_max, jnp.max(scores, axis=-1))
    rescale = jnp.exp(running_max - new_max)
    weights = jnp.exp(scores - new_max[:, :, None])
    if allowed is not None:
        weights = jnp.where(allowed, weights, 0.0)
    new_sum = running_sum * rescale + jnp.sum(weights, axis=-1)
    product = jnp.einsum(
        "htr,rhd->htd",
        weights.astype(jnp.bfloat16),
        value_block,
        preferred_element_type=jnp.float32,
    )
    return (new_max, new_sum, accum_out * rescale[:, :, None] + product)


def finish_rows(state_in):
    running_max, running_sum, accum_out = state_in
    output = accum_out / running_sum[:, :, None]
    head_count, row_count, head_size = output.shape
    return jnp.transpose(output, (1, 0, 2)).reshape(row_count, head_count * head_size)


def split_heads(rows_in, head_count):
    return rows_in.reshape(rows_in.shape[0], head_count, rows_in.shape[1] // head_count)


def shards(
    q_tok, k_tok, v_tok, strip_kv, bev_keys, bev_values, bev_list, bev_count, gate_table, timestep
):
    row_count = q_tok.shape[1]
    width = q_tok.shape[2]
    head_count = HEADS
    head_size = width // head_count
    queries = split_heads(q_tok[0], head_count)
    initial = (
        jnp.full((head_count, row_count), -1e30, jnp.float32),
        jnp.zeros((head_count, row_count), jnp.float32),
        jnp.zeros((head_count, row_count, head_size), jnp.float32),
    )
    key_piece = lax.all_gather(k_tok, "seq", axis=1, tiled=True)
    value_piece = lax.all_gather(v_tok, "seq", axis=1, tiled=True)
    piece_rows = key_piece.shape[1]
    stride = math.gcd(piece_rows, 512)
    key_heads = split_heads(key_piece[0], head_count)
    value_heads = split_heads(value_piece[0], head_count)

    def inner(block_idx, state_now):
        key_block = lax.dynamic_slice_in_dim(key_heads, block_idx * stride, stride, 0)
        value_block = lax.dynamic_slice_in_dim(value_heads, block_idx * stride, stride, 0)
        return online_step(state_now, queries, key_block, value_block, None)

    self_state = lax.fori_loop(0, piece_rows // stride, inner, initial)
    self_out = finish_rows(self_state)
    from_left = from_behind(strip_kv[:, 1], "cam", 1)
    from_right = from_behind(strip_kv[:, 0], "cam", -1)
    view_keys = jnp.concatenate([from_left[0, 0], from_right[0, 0]], axis=0)
    view_values = jnp.concatenate([from_left[0, 1], from_right[0, 1]], axis=0)
    view_out = finish_rows(
        online_step(
            initial,
            queries,
            split_heads(view_keys, head_count),
            split_heads(view_values, head_count),
            None,
        )
    )
    bev_rows = bev_keys.shape[0]
    listed_ids = bev_list[0, 0]
    used_count = bev_count[0, 0]
    all_keys, all_values = (
        lax.all_gather(bev_keys, "cam", axis=0, tiled=True),
        lax.all_gather(bev_values, "cam", axis=0, tiled=True),
    )
    picked_keys = jnp.concatenate(
        [
            lax.dynamic_slice_in_dim(all_keys, listed_ids[slot] * bev_rows, bev_rows, 0)
            for slot in range(LIST)
        ],
        axis=0,
    )
    picked_values = jnp.concatenate(
        [
            lax.dynamic_slice_in_dim(all_values, listed_ids[slot] * bev_rows, bev_rows, 0)
            for slot in range(LIST)
        ],
        axis=0,
    )
    slot_of = jnp.arange(LIST * bev_rows, dtype=jnp.int32) // bev_rows
    allowed = (slot_of < used_count)[None, None, :]
    bev_state = online_step(
        initial,
        queries,
        split_heads(picked_keys, head_count),
        split_heads(picked_values, head_count),
        allowed,
    )
    bev_out = finish_rows(bev_state)
    onehot = (jnp.arange(gate_table.shape[0], dtype=jnp.int32) == timestep[0]).astype(jnp.float32)
    gate_rows = jnp.tensordot(onehot, gate_table, axes=1, precision=lax.Precision.HIGHEST)
    blended = gate_rows[0] * self_out + gate_rows[1] * view_out + gate_rows[2] * bev_out
    return blended.astype(jnp.bfloat16).reshape(1, row_count, width)


def solution(mesh):
    return jax.shard_map(
        shards,
        mesh=mesh,
        in_specs=(
            P("cam", "seq", None),
            P("cam", "seq", None),
            P("cam", "seq", None),
            P("cam", None, None, "seq", None),
            P(("cam", "seq"), None),
            P(("cam", "seq"), None),
            P("cam", "seq", None),
            P("cam", "seq"),
            P(),
            P(),
        ),
        out_specs=P("cam", "seq", None),
        check_vma=False,
    )
```

profile of v0, /device:TPU:1, one launch (start us, length us, event | category | flops | bytes accessed | tf_op | source)
XLA Modules:
  0.0 391.6 jit_solution(8864212814673820211)
XLA Ops:
  12.6 4.0 %collective-permute-start.1 = (bf16[1,2,32,1536]{3,2,1,0:T(8,128)(2,1)S(1)}, bf16[1,2,32,1536]{3,2,1,0:T(8,128)(2,1)S(1)}, u32[]{:S(2)}, u32[]{:S(2)}) collective-permute-start(bf16[1,2,32,1536]{3,2,1,0:T(8,128)(2,1)S(1)} %get-tuple-element.184), channel_id=1, source_target_pairs={{0,224},{32,0},{64,32},{96,64},{128,96},{160,128},{192,160},{224,1... | collective-permute-start | bytes 589832 | tf_op jit(solution)/shard_map/ppermute | solution.py:14
  25.8 55.3 %all-gather.9.cloned.1.call-done = bf16[1024,1536]{1,0:T(8,128)(2,1)} async-done(((bf16[128,1536]{1,0:T(8,128)(2,1)}), bf16[1024,1536]{1,0:T(8,128)(2,1)}) %all-gather.9.cloned.1.call-update) | async-done | bytes 3145744 | tf_op jit(solution)/shard_map/all_gather | solution.py:95
  81.1 68.3 %all-gather.11.cloned.1.call-done = bf16[1024,1536]{1,0:T(8,128)(2,1)} async-done(((bf16[128,1536]{1,0:T(8,128)(2,1)}), bf16[1024,1536]{1,0:T(8,128)(2,1)}) %all-gather.11.cloned.1.call-update) | async-done | bytes 3145744 | tf_op jit(solution)/shard_map/all_gather | solution.py:96
  161.4 68.6 %all-gather.5.cloned.1.call-done = bf16[1,4096,1536]{2,1,0:T(8,128)(2,1)} async-done(((bf16[1,128,1536]{2,1,0:T(8,128)(2,1)}), bf16[1,4096,1536]{2,1,0:T(8,128)(2,1)}) %all-gather.5.cloned.1.call-update) | async-done | bytes 12582928 | tf_op jit(solution)/shard_map/all_gather | solution.py:64
  230.0 16.8 %copy.24 = bf16[1,4096,1536]{1,2,0:T(8,128)(2,1)} copy(bf16[1,4096,1536]{2,1,0:T(8,128)(2,1)} %all-gather.5.cloned.1.call-done) | data formatting | bytes 25165824 | tf_op jit(solution)/shard_map/all_gather | solution.py:64
  246.8 64.9 %all-gather.7.cloned.1.call-done = bf16[1,4096,1536]{2,1,0:T(8,128)(2,1)} async-done(((bf16[1,128,1536]{2,1,0:T(8,128)(2,1)}), bf16[1,4096,1536]{2,1,0:T(8,128)(2,1)}) %all-gather.7.cloned.1.call-update) | async-done | bytes 12582928 | tf_op jit(solution)/shard_map/all_gather | solution.py:65
  311.8 16.8 %copy.26 = bf16[1,4096,1536]{1,2,0:T(8,128)(2,1)} copy(bf16[1,4096,1536]{2,1,0:T(8,128)(2,1)} %all-gather.7.cloned.1.call-done) | data formatting | bytes 25165824 | tf_op jit(solution)/shard_map/all_gather | solution.py:65
  328.6 54.3 %while.18 = (s32[]{:T(128)}, f32[24,128]{1,0:T(8,128)S(1)}, f32[24,128]{1,0:T(8,128)S(1)}, f32[24,128,64]{1,2,0:T(8,128)S(1)}, bf16[4096,24,64]{0,2,1:T(8,128)(2...) while((s32[]{:T(128)}, f32[24,128]{1,0:T(8,128)S(1)}, ...), condition=%wide.region_3.0_spmd.clone, body=%wide.region_0.0_spmd.clone.sunk | while | flops 415841280 | bytes 24182968 | solution.py:76
  328.6 2.6 bitcast_reduce_fusion.3
  332.3 3.1 fusion.87
  335.5 2.6 bitcast_reduce_fusion.3
  339.1 3.1 fusion.87
  342.2 2.6 bitcast_reduce_fusion.3
  345.9 3.1 fusion.87
  349.0 2.6 bitcast_reduce_fusion.3
  352.7 3.1 fusion.87
  355.8 2.6 bitcast_reduce_fusion.3
  359.5 3.1 fusion.87
  362.6 2.6 bitcast_reduce_fusion.3
  366.3 3.1 fusion.87
  369.4 2.6 bitcast_reduce_fusion.3
  373.1 3.1 fusion.87
  376.2 2.6 bitcast_reduce_fusion.3
  379.9 3.1 fusion.87
  (87 shorter events, 34.5 us)
Async XLA Ops:
  6.5 14.8 %copy-start = (f32[50,3,1536]{2,0,1:T(8,128)S(1)}, f32[50,3,1536]{2,0,1:T(8,128)}, u32[]{:S(2)}) copy-start(f32[50,3,1536]{2,0,1:T(8,128)} %param.20) | copy-start | bytes 2764804
  6.5 74.5 %all-gather.9.cloned.1.call-start = ((), (), s32[]{:S(2)}) async-start(), calls=%async_computation.2 | async-start | bytes 3538944 | tf_op jit(solution)/shard_map/all_gather | solution.py:95
  7.3 142.1 %all-gather.11.cloned.1.call-start = ((), (), s32[]{:S(2)}) async-start(), calls=%async_computation.3 | async-start | bytes 3538944 | tf_op jit(solution)/shard_map/all_gather | solution.py:96
  8.0 222.0 %all-gather.5.cloned.1.call-start = ((), (), s32[]{:S(2)}) async-start(), calls=%async_computation | async-start | bytes 12976128 | tf_op jit(solution)/shard_map/all_gather | solution.py:64
  8.7 303.0 %all-gather.7.cloned.1.call-start = ((), (), s32[]{:S(2)}) async-start(), calls=%async_computation.1 | async-start | bytes 12976128 | tf_op jit(solution)/shard_map/all_gather | solution.py:65
  10.4 12.7 %collective-permute-start = (bf16[1,2,32,1536]{3,2,1,0:T(8,128)(2,1)S(1)}, bf16[1,2,32,1536]{3,2,1,0:T(8,128)(2,1)S(1)}, u32[]{:S(2)}, u32[]{:S(2)}) collective-permute-start(bf16[1,2,32,1536]{3,2,1,0:T(8,128)(2,1)S(1)} %get-tuple-element.183), channel_id=1, source_target_pairs={{0,32},{32,64},{64,96},{96,128},{128,160},{160,192},{192,224},{224... | collective-permute-start | bytes 589832 | tf_op jit(solution)/shard_map/ppermute | solution.py:14
  12.6 10.7 %collective-permute-start.1 = (bf16[1,2,32,1536]{3,2,1,0:T(8,128)(2,1)S(1)}, bf16[1,2,32,1536]{3,2,1,0:T(8,128)(2,1)S(1)}, u32[]{:S(2)}, u32[]{:S(2)}) collective-permute-start(bf16[1,2,32,1536]{3,2,1,0:T(8,128)(2,1)S(1)} %get-tuple-element.184), channel_id=1, source_target_pairs={{0,224},{32,0},{64,32},{96,64},{128,96},{160,128},{192,160},{224,1... | collective-permute-start | bytes 589832 | tf_op jit(solution)/shard_map/ppermute | solution.py:14
  155.9 3.8 copy-start.2
  328.6 54.5 %copy-start.3 = (f32[128,24,64]{0,2,1:T(8,128)S(1)}, f32[128,24,64]{0,2,1:T(8,128)}, u32[]{:S(2)}) copy-start(f32[128,24,64]{0,2,1:T(8,128)} %fusion.32) | copy-start | bytes 2359300
  383.0 2.1 copy-start.1
Sparse Core Ops, SparseCore 0:
  9.9 71.0 all-gather.8
  83.7 65.6 all-gather.10
  151.2 78.7 all-gather.4
  231.7 80.0 all-gather.6
where the time goes:
time: 393 us; the launch traced here: 392 us
  waiting for transfers between devices  260 us (66%)
  matrix products  51.5 us (13%)
  local copies, waits for them, and re-layouts  44.7 us (11%)
  between operations  16.7 us (4%)
  other arithmetic  12.3 us (3%)
  starting transfers between devices  6.31 us (2%)
    all_gather x1, waiting for transfers between devices, shards(): key_piece = lax.all_gather(k_tok, 'seq', axis=1, tiled=True)  68.6 us
    all_gather x1, waiting for transfers between devices, shards(): lax.all_gather(bev_values, 'cam', axis=0, tiled=True)  68.3 us
    all_gather x1, waiting for transfers between devices, shards(): value_piece = lax.all_gather(v_tok, 'seq', axis=1, tiled=True)  64.9 us
    all_gather x1, waiting for transfers between devices, shards(): lax.all_gather(bev_keys, 'cam', axis=0, tiled=True)  55.3 us
    dot_general x10, matrix products, online_step(): jnp.einsum('htr,rhd->htd', weights.astype(jnp.bfloat16), value_block, pre...  27.6 us
    dot_general x10, matrix products, online_step(): jnp.einsum('thd,rhd->htr', queries, key_block, preferred_element_type=jnp...  23.5 us
    all_gather x1, local copies, waits for them, and re-layouts, shards(): value_piece = lax.all_gather(v_tok, 'seq', axis=1, tiled=True)  16.8 us
    all_gather x1, local copies, waits for them, and re-layouts, shards(): key_piece = lax.all_gather(k_tok, 'seq', axis=1, tiled=True)  16.8 us
  transfers between devices with their start and end apart: 6, of which 4 were waited for; matrix products, arithmetic and copies ran while one was open for 9% of the time, Pallas kernels for 0%

commit v1 on v0

v1 whole, which is shorter than its diff:
```python
import functools
import math

import jax
import jax.numpy as jnp
from jax import lax
from jax.experimental import pallas as pl
from jax.experimental.pallas import tpu as pltpu
from jax.sharding import PartitionSpec as P

BF = jnp.bfloat16
F32 = jnp.float32
LANES = 128
HALF = 64
LIST = 3
NZ = 8
CAMS = 8
NY = 4
AWAY = ((0, 0), (1, 0), (0, 1), (0, 3), (1, 1), (0, 2), (1, 3), (1, 2))
PLACES = 2 * NZ
TOK = 128
EDGE = 32
WIDTH = 1536
KEYS = 4096
META = 16
BQ = 256
KT = 256
SCALE = math.log2(math.e) / math.sqrt(HALF)
NT = (((1,), (1,)), ((), ()))
VMEM_LIMIT = 56 * 2**20

Q_ONE = TOK
KV_TWO = Q_ONE + TOK // 2
Q_TWO = KV_TWO + TOK
Z_ROWS = Q_TWO + TOK // 4
O_ROWS = TOK // 2 + TOK // 4

C_V = TOK
C_ONE = 2 * TOK
C_Q = 3 * TOK
C_QONE = 4 * TOK
C_STRIP = C_QONE + TOK // 2
C_META = C_STRIP + 6 * EDGE
C_ROWS = C_META + META
CO_ROWS = TOK + TOK // 2


def low_lanes(rows):
    return lax.broadcasted_iota(jnp.int32, (rows, LANES), 1) < HALF


def half_turn(x):
    return pltpu.roll(x, HALF, 1)


def side_by_side(a, a_half, b, b_half):
    left = half_turn(a) if a_half else a
    right = b if b_half else half_turn(b)
    return jnp.where(low_lanes(a.shape[0]), left, right)


def folded(x, half):
    n = x.shape[0] // 2
    return side_by_side(x[:n], half, x[n:], half)


def tile(ref, index):
    return ref[:, index * LANES : (index + 1) * LANES]


def tile_at(ref, index):
    return ref[:, pl.ds(pl.multiple_of(index * LANES, LANES), LANES)]


def turned(x, flag):
    return jnp.where(flag, half_turn(x), x)


def cam_away(place, sign):
    cam = lax.axis_index("cam")
    x_hi, y = AWAY[place]
    x_hi = lax.rem(cam // NY + x_hi, 2)
    return x_hi * NY + lax.rem(lax.rem(cam, NY) + (y if sign > 0 else NY - y), NY)


def params():
    return pltpu.CompilerParams(vmem_limit_bytes=VMEM_LIMIT)


def pack_z_kernel(q_ref, k_ref, v_ref, out_ref):
    for z in range(NZ):
        at, half = NZ + z // 2, z % 2
        shared = side_by_side(tile(k_ref, at), half, tile(v_ref, at), half)
        q_shared = tile(q_ref, at)
        k, v, q = tile(k_ref, z), tile(v_ref, z), tile(q_ref, z)
        for x in range(2):
            place = 2 * z + x
            out_ref[place, :Q_ONE] = side_by_side(k, x, v, x)
            out_ref[place, Q_ONE:KV_TWO] = folded(q, x)
            out_ref[place, KV_TWO:Q_TWO] = shared
            out_ref[place, Q_TWO:] = folded(q_shared[x * HALF : (x + 1) * HALF], half)


def pack_cam_kernel(list_ref, count_ref, q_ref, k_ref, v_ref, strip_ref, *outs):
    lane = lax.broadcasted_iota(jnp.int32, (META, LANES), 1)
    uses = jnp.where(lane == LIST, count_ref[0, 0], 0)
    for j in range(LIST):
        uses = jnp.where(lane == j, list_ref[0, 0, j], uses)
    uses = uses.astype(F32).astype(BF)
    low = low_lanes(TOK)
    for i, out_ref in enumerate(outs):
        p = cam_away(i, 1)
        at = CAMS + p // 2
        odd = lax.rem(p, 2) == 1
        even = jnp.logical_not(odd)

        def third(k, v):
            first = turned(tile_at(k, at), odd)
            return jnp.where(low[: first.shape[0]], first, turned(tile_at(v, at), even))

        out_ref[:C_V] = tile_at(k_ref, p)
        out_ref[C_V:C_ONE] = tile_at(v_ref, p)
        out_ref[C_ONE:C_Q] = third(k_ref, v_ref)
        out_ref[C_Q:C_QONE] = tile_at(q_ref, p)
        q = tile_at(q_ref, at)
        out_ref[C_QONE:C_STRIP] = jnp.where(
            low[:HALF], turned(q[:HALF], odd), turned(q[HALF:], even)
        )
        for side in range(2):
            base = C_STRIP + side * EDGE
            k, v = strip_ref.at[side, 0], strip_ref.at[side, 1]
            out_ref[base : base + EDGE] = tile_at(k, p)
            out_ref[base + 2 * EDGE : base + 3 * EDGE] = tile_at(v, p)
            out_ref[base + 4 * EDGE : base + 5 * EDGE] = third(k, v)
        out_ref[C_META:] = uses


def self_kernel(mine_ref, other_ref, o_ref, kv_all, q_all, s_buf, m_buf, o_all):
    ones = jnp.ones((TOK, LANES), BF)
    for i, ref in enumerate((mine_ref, other_ref)):
        for place in range(PLACES):
            at = (i * PLACES + place) * TOK
            rows = slice(at, at + TOK)
            kv_all[0, rows, :LANES] = ref[place, :Q_ONE]
            kv_all[0, rows, LANES:] = ones
            kv_all[1, rows, :LANES] = ref[place, KV_TWO:Q_TWO]
            kv_all[1, rows, LANES:] = ones

    def unfold(q, at):
        n = q.shape[0]
        low, nil = low_lanes(n), jnp.zeros((n, LANES), BF)
        q_all[at : at + n] = jnp.where(low, q, nil)
        q_all[at + n : at + 2 * n] = jnp.where(low, half_turn(q), nil)

    first = PLACES * TOK
    for place in range(PLACES):
        unfold(mine_ref[place, Q_ONE:KV_TWO], place * TOK)
        unfold(mine_ref[place, Q_TWO:], first + place * HALF)
    steps = 3 * first // 2 // BQ

    def scores(i, slot):
        h = i // (first // BQ)
        q = q_all[pl.ds(pl.multiple_of(i * BQ, BQ), BQ)]
        largest = jnp.full((BQ, LANES), -jnp.inf, F32)
        for t in range(KEYS // KT):
            keys = kv_all[h, t * KT : (t + 1) * KT, :LANES]
            s = lax.dot_general(q, keys, NT, preferred_element_type=F32)
            s_buf[slot, :, t * KT : (t + 1) * KT] = s
            for j in range(KT // LANES):
                largest = jnp.maximum(largest, s[:, j * LANES : (j + 1) * LANES])
        top = jnp.max(largest, axis=1, keepdims=True) * SCALE
        m_buf[slot] = jnp.broadcast_to(top, (BQ, LANES))

    def values(i, slot):
        h = i // (first // BQ)
        top = jnp.concatenate([m_buf[slot]] * (KT // LANES), axis=1)
        total = jnp.zeros((BQ, 2 * LANES), F32)
        for t in range(KEYS // KT):
            s = s_buf[slot, :, t * KT : (t + 1) * KT]
            w = jnp.exp2(s * SCALE - top).astype(BF)
            total = total + jnp.dot(
                w, kv_all[h, t * KT : (t + 1) * KT], preferred_element_type=F32
            )
        o_all[pl.ds(pl.multiple_of(i * BQ, BQ), BQ)] = total[:, :LANES] / total[:, LANES:]

    scores(0, 0)

    def two_steps(j, carry):
        i = 2 * j
        scores(i + 1, 1)
        values(i, 0)
        scores(jnp.minimum(i + 2, steps - 1), 0)
        values(i + 1, 1)
        return carry

    lax.fori_loop(0, steps // 2, two_steps, 0)
    for place in range(PLACES):
        at = place * TOK
        o_ref[place, : TOK // 2] = folded(o_all[at : at + TOK], 1).astype(BF)
        at = first + place * HALF
        o_ref[place, TOK // 2 :] = folded(o_all[at : at + HALF], 1).astype(BF)


def attention(q, blocks, allowed=None):
    scores = []
    for j, (keys, _) in enumerate(blocks):
        s = lax.dot_general(q, keys, NT, preferred_element_type=F32) * SCALE
        if allowed is not None:
            s = jnp.where(allowed[j], s, -1e30)
        scores.append(s)
    top = functools.reduce(jnp.maximum, [jnp.max(s, axis=1, keepdims=True) for s in scores])
    total = jnp.zeros((q.shape[0], 2 * LANES), F32)
    for s, (_, vals) in zip(scores, blocks):
        w = jnp.exp2(s - top).astype(BF)
        wide = jnp.concatenate([vals, jnp.ones_like(vals)], axis=1)
        total = total + jnp.dot(w, wide, preferred_element_type=F32)
    return total[:, :LANES] / total[:, LANES:]


def cam_kernel(*refs):
    in_refs, gain_ref, o_ref = refs[:CAMS], refs[CAMS], refs[CAMS + 1]
    got_ref, uses_vec, uses_ref = refs[CAMS + 2 :]
    p = lax.axis_index("cam")
    for i in range(CAMS):
        got_ref[cam_away(i, -1)] = in_refs[i][...]
    for c in range(CAMS):
        uses = got_ref[c, C_META:].astype(F32)[:1].astype(jnp.int32)
        uses_vec[c : c + 1] = uses
    pltpu.sync_copy(uses_vec, uses_ref)

    def gain(row):
        pair = gain_ref[row : row + 1, pl.ds(pl.multiple_of(p * LANES, LANES), LANES)]
        at = CAMS + p // 2
        one = gain_ref[row : row + 1, pl.ds(pl.multiple_of(at * LANES, LANES), LANES)]
        one = jnp.broadcast_to(one, (8, LANES))
        return pair, jnp.where(lax.rem(p, 2) == 1, one, half_turn(one))[:1]

    view_gain, bev_gain = gain(1), gain(2)
    low, nil = low_lanes(TOK), jnp.zeros((TOK, LANES), BF)
    low_half, nil_half = low_lanes(HALF), jnp.zeros((HALF, LANES), BF)
    for c in range(CAMS):
        listed = [uses_ref[c, j] for j in range(LIST)]
        allowed = [j < uses_ref[c, LIST] for j in range(LIST)]
        left, right = (c - 1) % CAMS, (c + 1) % CAMS
        ends = ((left, C_STRIP + EDGE), (right, C_STRIP))

        def strips(part):
            return jnp.concatenate(
                [got_ref[e, at + part : at + part + EDGE] for e, at in ends], axis=0
            )

        q = got_ref[c, C_Q:C_QONE]
        q = jnp.concatenate([jnp.where(low, q, nil), jnp.where(low, nil, q)], axis=0)
        view = attention(q, [(strips(0), strips(2 * EDGE))])
        blocks = [(got_ref[e, :C_V], got_ref[e, C_V:C_ONE]) for e in listed]
        bev = attention(q, blocks, allowed)
        out = view * view_gain[0] + bev * bev_gain[0]
        o_ref[c, :TOK] = jnp.where(low, out[:TOK], out[TOK:]).astype(BF)

        q = got_ref[c, C_QONE:C_STRIP]
        q = jnp.concatenate(
            [jnp.where(low_half, q, nil_half), jnp.where(low_half, half_turn(q), nil_half)], axis=0
        )
        both = strips(4 * EDGE)
        view = attention(q, [(both, both)])
        blocks = [(got_ref[e, C_ONE:C_Q], got_ref[e, C_ONE:C_Q]) for e in listed]
        bev = attention(q, blocks, allowed)
        out = view * view_gain[1] + bev * bev_gain[1]
        o_ref[c, TOK:] = folded(out, 1).astype(BF)


def blend_kernel(self_ref, cam_ref, gain_ref, out_ref):
    def unfolded(x, y, n):
        lower = side_by_side(x, 0, y, 0)
        upper = side_by_side(x, 1, y, 1)
        return jnp.concatenate([lower, upper], axis=0)

    for i in range(WIDTH // LANES):
        cols = slice(i * LANES, (i + 1) * LANES)
        if i < NZ:
            one, two = (self_ref[2 * i + x, : TOK // 2].astype(F32) for x in range(2))
            mine = unfolded(one, two, HALF)
            other = cam_ref[i, :TOK].astype(F32)
        else:
            z = 2 * (i - NZ)
            parts = []
            for x in range(2):
                one, two = (self_ref[2 * (z + k) + x, TOK // 2 :].astype(F32) for k in range(2))
                parts.append(unfolded(one, two, HALF // 2))
            mine = jnp.concatenate(parts, axis=0)
            one, two = (cam_ref[z + k, TOK:].astype(F32) for k in range(2))
            other = unfolded(one, two, HALF)
        out_ref[:, cols] = (gain_ref[0:1, cols] * mine + other).astype(BF)


def of(shape, dtype=BF):
    return jax.ShapeDtypeStruct(shape, dtype)


def cost(flops, moved, exps):
    return pl.CostEstimate(flops=flops, bytes_accessed=moved, transcendentals=exps)


def after(x, *done):
    return lax.optimization_barrier((x,) + done)[0]


SAME_CORE = [[4 * z + 2 * x + c for z in range(NZ) for x in range(2)] for c in range(2)]


def z_exchange(x):
    return lax.all_to_all(x, "seq", 0, 0, axis_index_groups=SAME_CORE, tiled=True)


def cam_exchange(x):
    return lax.all_to_all(x, "cam", 0, 0, tiled=True)


def shards(
    q_tok, k_tok, v_tok, strip_kv, bev_keys, bev_values, bev_list, bev_count, gate_table, timestep
):
    q, k, v = q_tok[0], k_tok[0], v_tok[0]
    smem = pl.BlockSpec(memory_space=pltpu.SMEM)
    vmem = pl.BlockSpec(memory_space=pltpu.VMEM)
    gains = lax.dynamic_index_in_dim(gate_table, timestep[0], 0, keepdims=False)
    to_z = pl.pallas_call(
        pack_z_kernel,
        out_shape=of((PLACES, Z_ROWS, LANES)),
        compiler_params=params(),
        cost_estimate=cost(0, 2 * 6 * TOK * WIDTH, 0),
        name="pack_z",
    )(q, k, v)
    mine = z_exchange(to_z)
    to_cam = pl.pallas_call(
        pack_cam_kernel,
        out_shape=[of((C_ROWS, LANES))] * CAMS,
        in_specs=[smem] * 2 + [vmem] * 4,
        compiler_params=params(),
        cost_estimate=cost(0, 2 * 8 * TOK * WIDTH, 0),
        name="pack_cam",
    )(bev_list, bev_count, q, bev_keys, bev_values, strip_kv[0])
    got = [to_cam[0]]
    for i in range(1, CAMS):
        x_hi, y = AWAY[i]
        moves = [
            (NY * a + b, NY * ((a + x_hi) % 2) + (b + y) % NY) for a in range(2) for b in range(NY)
        ]
        got.append(lax.ppermute(to_cam[i], "cam", moves))
    mine = after(mine, *got)
    other = lax.ppermute(mine, "seq", [(s, s ^ 1) for s in range(4 * NZ)])
    cam_out = pl.pallas_call(
        cam_kernel,
        out_shape=of((CAMS, CO_ROWS, LANES)),
        scratch_shapes=[
            pltpu.VMEM((CAMS, C_ROWS, LANES), BF),
            pltpu.VMEM((CAMS, LANES), jnp.int32),
            pltpu.SMEM((CAMS, LANES), jnp.int32),
        ],
        compiler_params=params(),
        cost_estimate=cost(4 * 4 * TOK * 448 * WIDTH, 4 * TOK * WIDTH, TOK * 448 * 24),
        name="cam_attention",
    )(*got, gains)
    cam_back = cam_exchange(cam_out)
    self_out = pl.pallas_call(
        self_kernel,
        out_shape=of((PLACES, O_ROWS, LANES)),
        scratch_shapes=[
            pltpu.VMEM((2, KEYS, 2 * LANES), BF),
            pltpu.VMEM((3 * NZ * TOK, LANES), BF),
            pltpu.VMEM((2, BQ, KEYS), F32),
            pltpu.VMEM((2, BQ, LANES), F32),
            pltpu.VMEM((3 * NZ * TOK, LANES), F32),
        ],
        compiler_params=params(),
        cost_estimate=cost(4 * 4 * TOK * KEYS * WIDTH, 4 * KEYS * 384, TOK * KEYS * 24),
        name="self_attention",
    )(mine, other)
    self_back = z_exchange(self_out)
    blended = pl.pallas_call(
        blend_kernel,
        out_shape=of((TOK, WIDTH)),
        compiler_params=params(),
        cost_estimate=cost(0, 10 * TOK * WIDTH, 0),
        name="blend",
    )(self_back, cam_back, gains)
    return blended[None]


def solution(mesh):
    return jax.shard_map(
        shards,
        mesh=mesh,
        in_specs=(
            P("cam", "seq", None),
            P("cam", "seq", None),
            P("cam", "seq", None),
            P("cam", None, None, "seq", None),
            P(("cam", "seq"), None),
            P(("cam", "seq"), None),
            P("cam", "seq", None),
            P("cam", "seq"),
            P(),
            P(),
        ),
        out_specs=P("cam", "seq", None),
        check_vma=False,
    )
```

time: 393 us -> 113 us (0.29)
  waiting for transfers between devices: 260 us -> 17.9 us
  matrix products: 51.5 us -> 0 us
  local copies, waits for them, and re-layouts: 44.7 us -> 1.41 us
  Pallas kernels: 0 us -> 36.5 us
  starting transfers between devices: 6.31 us -> 33.9 us
  blocking collectives: 0 us -> 20.6 us
  between operations: 16.7 us -> 1.36 us
  other arithmetic: 12.3 us -> 0 us
    all_gather x4 -> x0, waiting for transfers between devices: 257 us -> none  [the longest x1 68.6 us: shards(): key_piece = lax.all_gather(k_tok, 'seq', axis=1, tiled=True)]
    dot_general x21 -> x0, matrix products: 51.5 us -> none  [the longest x10 27.6 us: online_step(): jnp.einsum('htr,rhd->htd', weights.astype(jnp.bfloat16), value_block, pre...]
    pallas_call x0 -> x5, Pallas kernels: none -> 36.5 us  [the longest x1 19.1 us: shards(): pl.pallas_call(self_kernel, out_shape=of((PLACES, O_ROWS, LANES)), scratc...]
    all_gather x2 -> x0, local copies, waits for them, and re-layouts: 33.7 us -> none  [the longest x1 16.8 us: shards(): value_piece = lax.all_gather(v_tok, 'seq', axis=1, tiled=True)]
    all_to_all x0 -> x1, blocking collectives: none -> 20.6 us  [z_exchange(): lax.all_to_all(x, 'seq', 0, 0, axis_index_groups=SAME_CORE, tiled=True)]
    ppermute x2 -> x8, waiting for transfers between devices: 0.01 us -> 17.9 us  [the longest x7 17.9 us: shards(): got.append(lax.ppermute(to_cam[i], 'cam', moves))]
    all_to_all x0 -> x2, starting transfers between devices: none -> 14 us  [the longest x1 10 us: z_exchange(): lax.all_to_all(x, 'seq', 0, 0, axis_index_groups=SAME_CORE, tiled=True)]
    ppermute x2 -> x8, starting transfers between devices: 6.19 us -> 19.8 us  [the longest x7 12.9 us: shards(): got.append(lax.ppermute(to_cam[i], 'cam', moves))]
  transfers between devices with their start and end apart: 6 -> 10, of which waited for: 4 -> 3; matrix products, arithmetic and copies ran while one was open for 9% -> 1% of each run, Pallas kernels for 0% -> 28%
where the time goes in v1:
time: 113 us; the launch traced here: 112 us
  Pallas kernels  36.5 us (32%)
  starting transfers between devices  33.9 us (30%)
  blocking collectives  20.6 us (18%)
  waiting for transfers between devices  17.9 us (16%)
  local copies, waits for them, and re-layouts  1.41 us (1%)
  between operations  1.36 us (1%)
    all_to_all x1, blocking collectives, z_exchange(): lax.all_to_all(x, 'seq', 0, 0, axis_index_groups=SAME_CORE, tiled=True)  20.6 us
    pallas_call x1, Pallas kernels, shards(): pl.pallas_call(self_kernel, out_shape=of((PLACES, O_ROWS, LANES)), scratc...  19.1 us
    ppermute x7, waiting for transfers between devices, shards(): got.append(lax.ppermute(to_cam[i], 'cam', moves))  17.9 us
    ppermute x7, starting transfers between devices, shards(): got.append(lax.ppermute(to_cam[i], 'cam', moves))  12.9 us
    all_to_all x1, starting transfers between devices, z_exchange(): lax.all_to_all(x, 'seq', 0, 0, axis_index_groups=SAME_CORE, tiled=True)  10 us
    pallas_call x1, Pallas kernels, shards(): pl.pallas_call(cam_kernel, out_shape=of((CAMS, CO_ROWS, LANES)), scratch_...  9.56 us
    ppermute x1, starting transfers between devices, shards(): other = lax.ppermute(mine, 'seq', [(s, s ^ 1) for s in range(4 * NZ)])  6.97 us
    all_to_all x1, starting transfers between devices, cam_exchange(): return lax.all_to_all(x, 'cam', 0, 0, tiled=True)  3.98 us
  transfers between devices with their start and end apart: 10, of which 3 were waited for; matrix products, arithmetic and copies ran while one was open for 1% of the time, Pallas kernels for 28%

profile of v1, /device:TPU:1, one launch (start us, length us, event | category | flops | bytes accessed | tf_op | source)
XLA Modules:
  0.0 111.7 jit_solution(16191642009183758505)
XLA Ops:
  0.0 2.8 %pack_z.1 = bf16[16,352,128]{2,1,0:T(8,128)(2,1)} custom-call(bf16[128,1536]{1,0:T(8,128)(2,1)} %bitcast.12, bf16[128,1536]{1,0:T(8,128)(2,1)} %bitcast.14, bf16[128,1536]{1,0:T(8,128)(2,1)} %bitcast.15), custom_call_target="tpu_custom_call" | custom-call | bytes 2359296 | tf_op jit(solution)/shard_map/pack_z/pallas_call | solution.py:326
  2.8 10.0 %all-to-all-start = ((bf16[16,352,128]{2,1,0:T(8,128)(2,1)}), bf16[16,352,128]{2,1,0:T(8,128)(2,1)S(1)}, u32[]{:S(2)}, u32[]{:S(2)}) async-start(bf16[16,352,128]{2,1,0:T(8,128)(2,1)} %pack_z.1), calls=%async_computation | async-start | bytes 2883584 | tf_op jit(solution)/shard_map/all_to_all | solution.py:312
  13.5 2.9 %pack_cam.1 = (bf16[784,128]{1,0:T(8,128)(2,1)}, bf16[784,128]{1,0:T(8,128)(2,1)}, bf16[784,128]{1,0:T(8,128)(2,1)}, bf16[784,128]{1,0:T(8,128)(2,1)}, bf16[784,...) custom-call(s32[1,1,3]{2,1,0:T(1,128)} %list_ref.1, ...), custom_call_target="tpu_custom_call" | custom-call | bytes 3145728 | tf_op jit(solution)/shard_map/pack_cam/pallas_call | solution.py:334
  16.5 2.4 %collective-permute-start = (bf16[784,128]{1,0:T(8,128)(2,1)}, bf16[784,128]{1,0:T(8,128)(2,1)S(1)}, u32[]{:S(2)}, u32[]{:S(2)}) collective-permute-start(bf16[784,128]{1,0:T(8,128)(2,1)} %get-tuple-element.15), channel_id=1, source_target_pairs={{0,128},{32,160},{64,192},{96,224},{128,0},{160,32},{192,64},{224,... | collective-permute-start | bytes 602120 | tf_op jit(solution)/shard_map/ppermute | solution.py:348
  18.9 1.3 %collective-permute-start.1 = (bf16[784,128]{1,0:T(8,128)(2,1)}, bf16[784,128]{1,0:T(8,128)(2,1)S(1)}, u32[]{:S(2)}, u32[]{:S(2)}) collective-permute-start(bf16[784,128]{1,0:T(8,128)(2,1)} %get-tuple-element.16), channel_id=1, source_target_pairs={{0,32},{32,64},{64,96},{96,0},{128,160},{160,192},{192,224},{224,1... | collective-permute-start | bytes 602120 | tf_op jit(solution)/shard_map/ppermute | solution.py:348
  20.2 1.4 %collective-permute-start.2 = (bf16[784,128]{1,0:T(8,128)(2,1)}, bf16[784,128]{1,0:T(8,128)(2,1)S(1)}, u32[]{:S(2)}, u32[]{:S(2)}) collective-permute-start(bf16[784,128]{1,0:T(8,128)(2,1)} %get-tuple-element.17), channel_id=1, source_target_pairs={{0,96},{32,0},{64,32},{96,64},{128,224},{160,128},{192,160},{224,1... | collective-permute-start | bytes 602120 | tf_op jit(solution)/shard_map/ppermute | solution.py:348
  21.6 0.3 collective-permute-start.3
  21.9 2.6 %collective-permute-start.4 = (bf16[784,128]{1,0:T(8,128)(2,1)}, bf16[784,128]{1,0:T(8,128)(2,1)S(1)}, u32[]{:S(2)}, u32[]{:S(2)}) collective-permute-start(bf16[784,128]{1,0:T(8,128)(2,1)} %get-tuple-element.19), channel_id=1, source_target_pairs={{0,64},{32,96},{64,0},{96,32},{128,192},{160,224},{192,128},{224,1... | collective-permute-start | bytes 602120 | tf_op jit(solution)/shard_map/ppermute | solution.py:348
  24.5 4.2 %collective-permute-start.5 = (bf16[784,128]{1,0:T(8,128)(2,1)}, bf16[784,128]{1,0:T(8,128)(2,1)S(1)}, u32[]{:S(2)}, u32[]{:S(2)}) collective-permute-start(bf16[784,128]{1,0:T(8,128)(2,1)} %get-tuple-element.20), channel_id=1, source_target_pairs={{0,224},{32,128},{64,160},{96,192},{128,96},{160,0},{192,32},{224,... | collective-permute-start | bytes 602120 | tf_op jit(solution)/shard_map/ppermute | solution.py:348
  28.8 0.0 collective-permute-done.1.refs_2_
  28.8 0.6 collective-permute-start.6
  29.3 0.0 collective-permute-done.2.refs_3_
  29.3 1.3 %collective-permute-done.3.refs_4_ = bf16[784,128]{1,0:T(8,128)(2,1)S(1)} collective-permute-done((bf16[784,128]{1,0:T(8,128)(2,1)}, bf16[784,128]{1,0:T(8,128)(2,1)S(1)}, u32[]{:S(2)}, u32[]{:S(2)}) %collective-permute-start.3) | collective-permute-done | bytes 200736 | tf_op jit(solution)/shard_map/ppermute | solution.py:348
  30.6 4.8 %collective-permute-done.4.refs_5_ = bf16[784,128]{1,0:T(8,128)(2,1)S(1)} collective-permute-done((bf16[784,128]{1,0:T(8,128)(2,1)}, bf16[784,128]{1,0:T(8,128)(2,1)S(1)}, u32[]{:S(2)}, u32[]{:S(2)}) %collective-permute-start.4) | collective-permute-done | bytes 200736 | tf_op jit(solution)/shard_map/ppermute | solution.py:348
  35.4 0.0 collective-permute-done.5.refs_6_
  35.4 0.7 copy-done.8
  36.1 11.9 %collective-permute-done.6.refs_7_ = bf16[784,128]{1,0:T(8,128)(2,1)} collective-permute-done((bf16[784,128]{1,0:T(8,128)(2,1)}, bf16[784,128]{1,0:T(8,128)(2,1)}, u32[]{:S(2)}, u32[]{:S(2)}) %collective-permute-start.6) | collective-permute-done | bytes 200736 | tf_op jit(solution)/shard_map/ppermute | solution.py:348
  48.0 7.0 %collective-permute-start.7 = (bf16[16,352,128]{2,1,0:T(8,128)(2,1)S(1)}, bf16[16,352,128]{2,1,0:T(8,128)(2,1)}, u32[]{:S(2)}, u32[]{:S(2)}) collective-permute-start(bf16[16,352,128]{2,1,0:T(8,128)(2,1)S(1)} %all-to-all-done.mine_ref), channel_id=1, source_target_pairs={{0,1},{1,0},{2,3},{3,2},{4,5},{5,4},{6,7},{7,6},{8,9},{9,8},{10,11... | collective-permute-start | bytes 4325384 | tf_op jit(solution)/shard_map/ppermute | solution.py:350
  55.7 0.6 copy.13
  56.3 9.6 %cam_attention.1 = bf16[8,192,128]{2,1,0:T(8,128)(2,1)} custom-call(bf16[784,128]{1,0:T(8,128)(2,1)} %get-tuple-element.14.refs_0_, bf16[784,128]{1,0:T(8,128)(2,1)} %copy-done.3, bf16[784,128]{1,0:T(8,128)(2,1)} %copy-done.4, bf16[784,128]{1,0:T(8,128)(2,1)} %copy-done.5, bf16[784,128]{1,0:T(8,128)(2,1)} %copy-done.6, bf16[784,128]{1,0:T(8,128)(2,1)} %copy-done.7, ...), custom_call_target="tpu_custom_call" | custom-call | flops 1409286144 | bytes 786432 | tf_op jit(solution)/shard_map/cam_attention/pallas_call | solution.py:351
  65.9 4.0 %all-to-all-start.2 = ((bf16[8,192,128]{2,1,0:T(8,128)(2,1)}), bf16[8,192,128]{2,1,0:T(8,128)(2,1)S(1)}, u32[]{:S(2)}, u32[]{:S(2)}) async-start(bf16[8,192,128]{2,1,0:T(8,128)(2,1)} %cam_attention.1), calls=%async_computation.2 | async-start | bytes 786432 | tf_op jit(solution)/shard_map/all_to_all | solution.py:316
  69.9 19.1 %self_attention.1 = bf16[16,96,128]{2,1,0:T(8,128)(2,1)} custom-call(bf16[16,352,128]{2,1,0:T(8,128)(2,1)} %copy-done.2, bf16[16,352,128]{2,1,0:T(8,128)(2,1)} %collective-permute-done.7.other_ref), custom_call_target="tpu_custom_call" | custom-call | flops 12884901888 | bytes 6291456 | tf_op jit(solution)/shard_map/self_attention/pallas_call | solution.py:364
  89.0 20.6 %all_to_all.15.self_ref = bf16[16,96,128]{2,1,0:T(8,128)(2,1)} all-to-all(bf16[16,96,128]{2,1,0:T(8,128)(2,1)} %self_attention.1), channel_id=1, replica_groups={{0,2,4,6,8,10,12,14,16,18,20,22,24,26,28,30},{1,3,5,7,9,11,13,15,17,19,..., dimensions={0} | all-to-all | bytes 786432 | tf_op jit(solution)/shard_map/all_to_all | solution.py:312
  109.5 2.1 %blend.1 = bf16[128,1536]{1,0:T(8,128)(2,1)} custom-call(bf16[16,96,128]{2,1,0:T(8,128)(2,1)} %all_to_all.15.self_ref, bf16[8,192,128]{2,1,0:T(8,128)(2,1)} %copy-done.1, f32[3,1536]{1,0:T(4,128)} %bitcast.18), custom_call_target="tpu_custom_call" | custom-call | bytes 1966080 | tf_op jit(solution)/shard_map/blend/pallas_call | solution.py:379
  (22 shorter events, 0.1 us)
Async XLA Ops:
  0.0 55.6 %copy-start = (f32[50,3,1536]{2,0,1:T(8,128)S(1)}, f32[50,3,1536]{2,0,1:T(8,128)}, u32[]{:S(2)}) copy-start(f32[50,3,1536]{2,0,1:T(8,128)} %param.18) | copy-start | bytes 2764804
  2.8 45.2 %all-to-all-start = ((bf16[16,352,128]{2,1,0:T(8,128)(2,1)}), bf16[16,352,128]{2,1,0:T(8,128)(2,1)S(1)}, u32[]{:S(2)}, u32[]{:S(2)}) async-start(bf16[16,352,128]{2,1,0:T(8,128)(2,1)} %pack_z.1), calls=%async_computation | async-start | bytes 2883584 | tf_op jit(solution)/shard_map/all_to_all | solution.py:312
  16.5 8.1 %collective-permute-start = (bf16[784,128]{1,0:T(8,128)(2,1)}, bf16[784,128]{1,0:T(8,128)(2,1)S(1)}, u32[]{:S(2)}, u32[]{:S(2)}) collective-permute-start(bf16[784,128]{1,0:T(8,128)(2,1)} %get-tuple-element.15), channel_id=1, source_target_pairs={{0,128},{32,160},{64,192},{96,224},{128,0},{160,32},{192,64},{224,... | collective-permute-start | bytes 602120 | tf_op jit(solution)/shard_map/ppermute | solution.py:348
  18.9 9.9 %collective-permute-start.1 = (bf16[784,128]{1,0:T(8,128)(2,1)}, bf16[784,128]{1,0:T(8,128)(2,1)S(1)}, u32[]{:S(2)}, u32[]{:S(2)}) collective-permute-start(bf16[784,128]{1,0:T(8,128)(2,1)} %get-tuple-element.16), channel_id=1, source_target_pairs={{0,32},{32,64},{64,96},{96,0},{128,160},{160,192},{192,224},{224,1... | collective-permute-start | bytes 602120 | tf_op jit(solution)/shard_map/ppermute | solution.py:348
  20.2 9.1 %collective-permute-start.2 = (bf16[784,128]{1,0:T(8,128)(2,1)}, bf16[784,128]{1,0:T(8,128)(2,1)S(1)}, u32[]{:S(2)}, u32[]{:S(2)}) collective-permute-start(bf16[784,128]{1,0:T(8,128)(2,1)} %get-tuple-element.17), channel_id=1, source_target_pairs={{0,96},{32,0},{64,32},{96,64},{128,224},{160,128},{192,160},{224,1... | collective-permute-start | bytes 602120 | tf_op jit(solution)/shard_map/ppermute | solution.py:348
  21.6 9.0 %collective-permute-start.3 = (bf16[784,128]{1,0:T(8,128)(2,1)}, bf16[784,128]{1,0:T(8,128)(2,1)S(1)}, u32[]{:S(2)}, u32[]{:S(2)}) collective-permute-start(bf16[784,128]{1,0:T(8,128)(2,1)} %get-tuple-element.18), channel_id=1, source_target_pairs={{0,160},{32,192},{64,224},{96,128},{128,32},{160,64},{192,96},{224... | collective-permute-start | bytes 602120 | tf_op jit(solution)/shard_map/ppermute | solution.py:348
  21.9 13.5 %collective-permute-start.4 = (bf16[784,128]{1,0:T(8,128)(2,1)}, bf16[784,128]{1,0:T(8,128)(2,1)S(1)}, u32[]{:S(2)}, u32[]{:S(2)}) collective-permute-start(bf16[784,128]{1,0:T(8,128)(2,1)} %get-tuple-element.19), channel_id=1, source_target_pairs={{0,64},{32,96},{64,0},{96,32},{128,192},{160,224},{192,128},{224,1... | collective-permute-start | bytes 602120 | tf_op jit(solution)/shard_map/ppermute | solution.py:348
  24.5 31.8 %copy-start.3 = (bf16[784,128]{1,0:T(8,128)(2,1)}, bf16[784,128]{1,0:T(8,128)(2,1)S(1)}, u32[]{:S(2)}) copy-start(bf16[784,128]{1,0:T(8,128)(2,1)S(1)} %collective-permute-done.refs_1_) | copy-start | bytes 602116
  24.5 10.8 %collective-permute-start.5 = (bf16[784,128]{1,0:T(8,128)(2,1)}, bf16[784,128]{1,0:T(8,128)(2,1)S(1)}, u32[]{:S(2)}, u32[]{:S(2)}) collective-permute-start(bf16[784,128]{1,0:T(8,128)(2,1)} %get-tuple-element.20), channel_id=1, source_target_pairs={{0,224},{32,128},{64,160},{96,192},{128,96},{160,0},{192,32},{224,... | collective-permute-start | bytes 602120 | tf_op jit(solution)/shard_map/ppermute | solution.py:348
  28.8 27.5 %copy-start.4 = (bf16[784,128]{1,0:T(8,128)(2,1)}, bf16[784,128]{1,0:T(8,128)(2,1)S(1)}, u32[]{:S(2)}) copy-start(bf16[784,128]{1,0:T(8,128)(2,1)S(1)} %collective-permute-done.1.refs_2_) | copy-start | bytes 602116
  28.8 19.2 %collective-permute-start.6 = (bf16[784,128]{1,0:T(8,128)(2,1)}, bf16[784,128]{1,0:T(8,128)(2,1)}, u32[]{:S(2)}, u32[]{:S(2)}) collective-permute-start(bf16[784,128]{1,0:T(8,128)(2,1)} %get-tuple-element.21), channel_id=1, source_target_pairs={{0,192},{32,224},{64,128},{96,160},{128,64},{160,96},{192,0},{224,... | collective-permute-start | bytes 602120 | tf_op jit(solution)/shard_map/ppermute | solution.py:348
  29.3 27.0 %copy-start.5 = (bf16[784,128]{1,0:T(8,128)(2,1)}, bf16[784,128]{1,0:T(8,128)(2,1)S(1)}, u32[]{:S(2)}) copy-start(bf16[784,128]{1,0:T(8,128)(2,1)S(1)} %collective-permute-done.2.refs_3_) | copy-start | bytes 602116
  30.6 25.7 %copy-start.6 = (bf16[784,128]{1,0:T(8,128)(2,1)}, bf16[784,128]{1,0:T(8,128)(2,1)S(1)}, u32[]{:S(2)}) copy-start(bf16[784,128]{1,0:T(8,128)(2,1)S(1)} %collective-permute-done.3.refs_4_) | copy-start | bytes 602116
  35.4 20.9 %copy-start.7 = (bf16[784,128]{1,0:T(8,128)(2,1)}, bf16[784,128]{1,0:T(8,128)(2,1)S(1)}, u32[]{:S(2)}) copy-start(bf16[784,128]{1,0:T(8,128)(2,1)S(1)} %collective-permute-done.4.refs_5_) | copy-start | bytes 602116
  35.4 0.7 copy-start.8
  48.0 17.9 %copy-start.2 = (bf16[16,352,128]{2,1,0:T(8,128)(2,1)}, bf16[16,352,128]{2,1,0:T(8,128)(2,1)S(1)}, u32[]{:S(2)}) copy-start(bf16[16,352,128]{2,1,0:T(8,128)(2,1)S(1)} %all-to-all-done.mine_ref) | copy-start | bytes 4325380
  48.0 21.9 %collective-permute-start.7 = (bf16[16,352,128]{2,1,0:T(8,128)(2,1)S(1)}, bf16[16,352,128]{2,1,0:T(8,128)(2,1)}, u32[]{:S(2)}, u32[]{:S(2)}) collective-permute-start(bf16[16,352,128]{2,1,0:T(8,128)(2,1)S(1)} %all-to-all-done.mine_ref), channel_id=1, source_target_pairs={{0,1},{1,0},{2,3},{3,2},{4,5},{5,4},{6,7},{7,6},{8,9},{9,8},{10,11... | collective-permute-start | bytes 4325384 | tf_op jit(solution)/shard_map/ppermute | solution.py:350
  65.9 23.1 %all-to-all-start.2 = ((bf16[8,192,128]{2,1,0:T(8,128)(2,1)}), bf16[8,192,128]{2,1,0:T(8,128)(2,1)S(1)}, u32[]{:S(2)}, u32[]{:S(2)}) async-start(bf16[8,192,128]{2,1,0:T(8,128)(2,1)} %cam_attention.1), calls=%async_computation.2 | async-start | bytes 786432 | tf_op jit(solution)/shard_map/all_to_all | solution.py:316
  88.9 20.6 %copy-start.1 = (bf16[8,192,128]{2,1,0:T(8,128)(2,1)}, bf16[8,192,128]{2,1,0:T(8,128)(2,1)S(1)}, u32[]{:S(2)}) copy-start(bf16[8,192,128]{2,1,0:T(8,128)(2,1)S(1)} %all-to-all-done.2.cam_ref) | copy-start | bytes 1179652

commit v2 on v1

v2 whole, which is shorter than its diff:
```python
import functools
import math

import jax
import jax.numpy as jnp
from jax import lax
from jax.experimental import pallas as pl
from jax.experimental.pallas import tpu as pltpu
from jax.sharding import PartitionSpec as P

BF = jnp.bfloat16
F32 = jnp.float32
LANES = 128
HALF = 64
LIST = 3
NZ = 8
CAMS = 8
NY = 4
GROUP_PAIRS = 3
GROUP_COLS = GROUP_PAIRS * 128
PLACES = 2 * NZ
TOK = 128
EDGE = 32
WIDTH = 1536
KEYS = 4096
META = 16
BQ = 256
KT = 256
V_ROWS = 80
SCALE = math.log2(math.e) / math.sqrt(HALF)
NT = (((1,), (1,)), ((), ()))
VMEM_LIMIT = 56 * 2**20

Q_ONE = TOK
KV_TWO = Q_ONE + TOK // 2
Q_TWO = KV_TWO + TOK
Z_ROWS = Q_TWO + TOK // 4
O_ROWS = TOK // 2 + TOK // 4

C_V = TOK
C_Q = 2 * TOK
C_META = 3 * TOK
C_ROWS = C_META + META


def low_lanes(rows):
    return lax.broadcasted_iota(jnp.int32, (rows, LANES), 1) < HALF


def half_turn(x):
    return pltpu.roll(x, HALF, 1)


def side_by_side(a, a_half, b, b_half):
    left = half_turn(a) if a_half else a
    right = b if b_half else half_turn(b)
    return jnp.where(low_lanes(a.shape[0]), left, right)


def folded(x, half):
    n = x.shape[0] // 2
    return side_by_side(x[:n], half, x[n:], half)


def tile(ref, index):
    return ref[:, index * LANES : (index + 1) * LANES]


def params():
    return pltpu.CompilerParams(vmem_limit_bytes=VMEM_LIMIT)


def pack_z_kernel(q_ref, k_ref, v_ref, out_ref):
    for z in range(NZ):
        at, half = NZ + z // 2, z % 2
        shared = side_by_side(tile(k_ref, at), half, tile(v_ref, at), half)
        q_shared = tile(q_ref, at)
        k, v, q = tile(k_ref, z), tile(v_ref, z), tile(q_ref, z)
        for x in range(2):
            place = 2 * z + x
            out_ref[place, :Q_ONE] = side_by_side(k, x, v, x)
            out_ref[place, Q_ONE:KV_TWO] = folded(q, x)
            out_ref[place, KV_TWO:Q_TWO] = shared
            out_ref[place, Q_TWO:] = folded(q_shared[x * HALF : (x + 1) * HALF], half)


def pack_cam_kernel(list_ref, count_ref, q_ref, k_ref, v_ref, *outs):
    y = lax.rem(lax.axis_index("cam"), NY)
    lane = lax.broadcasted_iota(jnp.int32, (META, GROUP_COLS), 1)
    uses = jnp.where(lane == LIST, count_ref[0, 0], 0)
    for j in range(LIST):
        uses = jnp.where(lane == j, list_ref[0, 0, j], uses)
    uses = uses.astype(F32).astype(BF)
    for d, out_ref in enumerate(outs):
        cols = pl.ds(pl.multiple_of(lax.rem(y + d, NY) * GROUP_COLS, LANES), GROUP_COLS)
        out_ref[:C_V] = k_ref[:, cols]
        out_ref[C_V:C_Q] = v_ref[:, cols]
        out_ref[C_Q:C_META] = q_ref[:, cols]
        out_ref[C_META:] = uses


def self_kernel(mine_ref, other_ref, o_ref, v_all, q_all, s_buf, m_buf, o_all):
    both = (mine_ref, other_ref)
    for i, ref in enumerate(both):
        for place in range(PLACES):
            cols = slice((i * PLACES + place) * TOK, (i * PLACES + place + 1) * TOK)
            v_all[0, :HALF, cols] = ref[place, :TOK].T[HALF:]
            v_all[1, :HALF, cols] = ref[place, KV_TWO:Q_TWO].T[HALF:]
    v_all[:, HALF:] = jnp.ones((2, V_ROWS - HALF, KEYS), BF)

    def unfold(q, at):
        n = q.shape[0]
        low, nil = low_lanes(n), jnp.zeros((n, LANES), BF)
        q_all[at : at + n] = jnp.where(low, q, nil)
        q_all[at + n : at + 2 * n] = jnp.where(low, half_turn(q), nil)

    first = PLACES * TOK
    for place in range(PLACES):
        unfold(mine_ref[place, Q_ONE:KV_TWO], place * TOK)
        unfold(mine_ref[place, Q_TWO:], first + place * HALF)
    change = first // BQ
    steps = change + change // 2

    def scores(i, slot):
        rows = pl.ds(pl.multiple_of(i // change * KV_TWO, HALF), TOK)
        q = q_all[pl.ds(pl.multiple_of(i * BQ, BQ), BQ)]
        largest = jnp.full((8, BQ), -jnp.inf, F32)
        for t in range(2 * PLACES):
            keys = both[t // PLACES][t % PLACES, rows]
            s = lax.dot_general(keys, q, NT, preferred_element_type=F32)
            s_buf[slot, t * TOK : (t + 1) * TOK] = s
            largest = jnp.maximum(largest, jnp.max(s.reshape(TOK // 8, 8, BQ), axis=0))
        top = jnp.max(largest, axis=0, keepdims=True) * SCALE
        m_buf[slot] = jnp.broadcast_to(top, (8, BQ))

    def values(i, slot):
        top = m_buf[slot][:1]
        total = jnp.zeros((V_ROWS, BQ), F32)
        for t in range(KEYS // KT):
            s = s_buf[slot, t * KT : (t + 1) * KT]
            w = jnp.exp2(s * SCALE - top).astype(BF)
            total = total + jnp.dot(
                v_all[i // change, :, t * KT : (t + 1) * KT], w, preferred_element_type=F32
            )
        out = total[:HALF] / total[HALF : HALF + 1]
        out = jnp.concatenate([out, out], axis=0).T
        o_all[pl.ds(pl.multiple_of(i * BQ, BQ), BQ)] = out

    scores(0, 0)

    def two_steps(j, carry):
        i = 2 * j
        scores(i + 1, 1)
        values(i, 0)
        scores(jnp.minimum(i + 2, steps - 1), 0)
        values(i + 1, 1)
        return carry

    lax.fori_loop(0, steps // 2, two_steps, 0)

    def fold(at, n):
        return jnp.where(low_lanes(n), o_all[at : at + n], o_all[at + n : at + 2 * n]).astype(BF)

    for place in range(PLACES):
        o_ref[place, : TOK // 2] = fold(place * TOK, TOK // 2)
        o_ref[place, TOK // 2 :] = fold(first + place * HALF, TOK // 4)


def attention(q, blocks, allowed=None):
    scores = [lax.dot_general(q, keys, NT, preferred_element_type=F32) for keys, _ in blocks]
    if allowed is not None:
        scores = [jnp.where(ok, s, -1e30) for ok, s in zip(allowed, scores)]
    top = jnp.max(functools.reduce(jnp.maximum, scores), axis=1, keepdims=True) * SCALE
    weights = jnp.concatenate([jnp.exp2(s * SCALE - top).astype(BF) for s in scores], axis=1)
    wide = jnp.concatenate([v for _, v in blocks], axis=0)
    wide = jnp.concatenate([wide, jnp.ones_like(wide)], axis=1)
    total = jnp.dot(weights, wide, preferred_element_type=F32)
    return total[:, :LANES] / total[:, LANES:]


def pair_attention(q, blocks, allowed=None):
    low, nil = low_lanes(TOK), jnp.zeros_like(q)
    both = jnp.concatenate([jnp.where(low, q, nil), jnp.where(low, nil, q)], axis=0)
    out = attention(both, blocks, allowed)
    return jnp.where(low, out[:TOK], out[TOK:])


def view_kernel(q_ref, left_ref, right_ref, out_ref):
    for i in range(WIDTH // LANES):
        cols = slice(i * LANES, (i + 1) * LANES)
        keys = jnp.concatenate([left_ref[0, :, cols], right_ref[0, :, cols]], axis=0)
        vals = jnp.concatenate([left_ref[1, :, cols], right_ref[1, :, cols]], axis=0)
        out_ref[:, cols] = pair_attention(q_ref[:, cols], [(keys, vals)])


def layout_kernel(*refs):
    in_refs, far_ref, o_refs = refs[:NY], refs[NY], refs[NY + 1 : 2 * NY + 1]
    kv_all, uses_vec, uses_ref = refs[2 * NY + 1 :]
    cam = lax.axis_index("cam")
    x_hi, y = cam // NY, lax.rem(cam, NY)
    for d in range(NY):
        uses_vec[d : d + 1] = in_refs[d][C_META:, :LANES].astype(F32)[:1].astype(jnp.int32)
    uses_vec[NY:] = jnp.zeros((NY, LANES), jnp.int32)
    pltpu.sync_copy(uses_vec, uses_ref)
    for d in range(NY):
        kv_all[d] = in_refs[d][:C_Q]
        kv_all[NY + d] = far_ref[d * C_Q : (d + 1) * C_Q]
    for d in range(NY):
        places, allowed = [], []
        for j in range(LIST):
            e = uses_ref[d, j]
            place = lax.rem(y - lax.rem(e, NY) + NY, NY)
            places.append(jnp.where(e // NY == x_hi, place, place + NY))
            allowed.append(j < uses_ref[d, LIST])
        for p in range(GROUP_PAIRS):
            cols = slice(p * LANES, (p + 1) * LANES)
            blocks = [(kv_all[e, :C_V, cols], kv_all[e, C_V:, cols]) for e in places]
            q = in_refs[d][C_Q:C_META, cols]
            o_refs[d][:, cols] = pair_attention(q, blocks, allowed).astype(BF)


def blend_kernel(self_ref, *refs):
    cam_refs = refs[:NY]
    view_ref, gain_ref, out_ref, cam_all = refs[NY:]
    y = lax.rem(lax.axis_index("cam"), NY)
    for d in range(NY):
        cam_all[lax.rem(y + d, NY)] = cam_refs[d][...]

    def unfolded(x, y, n):
        lower = side_by_side(x, 0, y, 0)
        upper = side_by_side(x, 1, y, 1)
        return jnp.concatenate([lower, upper], axis=0)

    for i in range(WIDTH // LANES):
        cols = slice(i * LANES, (i + 1) * LANES)
        if i < NZ:
            one, two = (self_ref[2 * i + x, : TOK // 2].astype(F32) for x in range(2))
            mine = unfolded(one, two, HALF)
        else:
            z = 2 * (i - NZ)
            parts = []
            for x in range(2):
                one, two = (self_ref[2 * (z + k) + x, TOK // 2 :].astype(F32) for k in range(2))
                parts.append(unfolded(one, two, HALF // 2))
            mine = jnp.concatenate(parts, axis=0)
        at = i % GROUP_PAIRS
        other = cam_all[i // GROUP_PAIRS, :, at * LANES : (at + 1) * LANES].astype(F32)
        blended = gain_ref[0:1, cols] * mine + gain_ref[1:2, cols] * view_ref[:, cols]
        out_ref[:, cols] = (blended + gain_ref[2:3, cols] * other).astype(BF)


def of(shape, dtype=BF):
    return jax.ShapeDtypeStruct(shape, dtype)


def cost(flops, moved, exps):
    return pl.CostEstimate(flops=flops, bytes_accessed=moved, transcendentals=exps)


def after(x, *done):
    return lax.optimization_barrier((x,) + done)[0]


SAME_CORE = [[4 * z + 2 * x + c for z in range(NZ) for x in range(2)] for c in range(2)]


def z_exchange(x):
    return lax.all_to_all(x, "seq", 0, 0, axis_index_groups=SAME_CORE, tiled=True)


def y_send(x, by):
    moves = [(NY * a + b, NY * a + (b + by) % NY) for a in range(2) for b in range(NY)]
    return lax.ppermute(x, "cam", moves)


def shards(
    q_tok, k_tok, v_tok, strip_kv, bev_keys, bev_values, bev_list, bev_count, gate_table, timestep
):
    q, k, v = q_tok[0], k_tok[0], v_tok[0]
    smem = pl.BlockSpec(memory_space=pltpu.SMEM)
    vmem = pl.BlockSpec(memory_space=pltpu.VMEM)
    gains = lax.dynamic_index_in_dim(gate_table, timestep[0], 0, keepdims=False)
    to_z = pl.pallas_call(
        pack_z_kernel,
        out_shape=of((PLACES, Z_ROWS, LANES)),
        compiler_params=params(),
        cost_estimate=cost(0, 2 * 6 * TOK * WIDTH, 0),
        name="pack_z",
    )(q, k, v)
    mine = z_exchange(to_z)
    to_cam = pl.pallas_call(
        pack_cam_kernel,
        out_shape=[of((C_ROWS, GROUP_COLS))] * NY,
        in_specs=[smem] * 2 + [vmem] * 3,
        compiler_params=params(),
        cost_estimate=cost(0, 2 * 6 * TOK * WIDTH, 0),
        name="pack_cam",
    )(bev_list, bev_count, q, bev_keys, bev_values)
    got = [to_cam[0]] + [y_send(to_cam[d], d) for d in range(1, NY)]
    ring = range(CAMS)
    from_left = lax.ppermute(strip_kv[0, 1], "cam", [(c, (c + 1) % CAMS) for c in ring])
    from_right = lax.ppermute(strip_kv[0, 0], "cam", [(c, (c - 1) % CAMS) for c in ring])
    view = pl.pallas_call(
        view_kernel,
        out_shape=of((TOK, WIDTH), F32),
        compiler_params=params(),
        cost_estimate=cost(16 * TOK * 64 * WIDTH, 4 * TOK * WIDTH, TOK * 64 * 24),
        name="view_attention",
    )(q, from_left, from_right)
    to_far = jnp.concatenate([t[:C_Q] for t in got], axis=0)
    far = lax.ppermute(to_far, "cam", [(c, (c + NY) % CAMS) for c in ring])
    mine = after(mine, view, to_far)
    other = lax.ppermute(mine, "seq", [(s, s ^ 1) for s in range(4 * NZ)])
    queries = 3 * NZ * TOK
    self_out = pl.pallas_call(
        self_kernel,
        out_shape=of((PLACES, O_ROWS, LANES)),
        scratch_shapes=[
            pltpu.VMEM((2, V_ROWS, KEYS), BF),
            pltpu.VMEM((queries, LANES), BF),
            pltpu.VMEM((2, KEYS, BQ), F32),
            pltpu.VMEM((2, 8, BQ), F32),
            pltpu.VMEM((queries, LANES), F32),
        ],
        compiler_params=params(),
        cost_estimate=cost(16 * queries * KEYS * HALF, 8 * KEYS * LANES, queries * KEYS),
        name="self_attention",
    )(mine, other)
    self_back = z_exchange(self_out)
    far = after(far, self_out)
    layout_out = pl.pallas_call(
        layout_kernel,
        out_shape=[of((TOK, GROUP_COLS))] * NY,
        scratch_shapes=[
            pltpu.VMEM((CAMS, C_Q, GROUP_COLS), BF),
            pltpu.VMEM((CAMS, LANES), jnp.int32),
            pltpu.SMEM((CAMS, LANES), jnp.int32),
        ],
        compiler_params=params(),
        cost_estimate=cost(16 * TOK * 384 * WIDTH, 4 * TOK * WIDTH, TOK * 384 * 24),
        name="layout_attention",
    )(*got, far)
    cam_back = [layout_out[0]] + [y_send(layout_out[d], NY - d) for d in range(1, NY)]
    blended = pl.pallas_call(
        blend_kernel,
        out_shape=of((TOK, WIDTH)),
        scratch_shapes=[pltpu.VMEM((NY, TOK, GROUP_COLS), BF)],
        compiler_params=params(),
        cost_estimate=cost(0, 10 * TOK * WIDTH, 0),
        name="blend",
    )(self_back, *cam_back, view, gains)
    return blended[None]


def solution(mesh):
    return jax.shard_map(
        shards,
        mesh=mesh,
        in_specs=(
            P("cam", "seq", None),
            P("cam", "seq", None),
            P("cam", "seq", None),
            P("cam", None, None, "seq", None),
            P(("cam", "seq"), None),
            P(("cam", "seq"), None),
            P("cam", "seq", None),
            P("cam", "seq"),
            P(),
            P(),
        ),
        out_specs=P("cam", "seq", None),
        check_vma=False,
    )
```

time: 113 us -> 97.7 us (0.86)
  blocking collectives: 20.6 us -> 0 us
  local copies, waits for them, and re-layouts: 1.41 us -> 5.09 us
  starting transfers between devices: 33.9 us -> 36 us
  waiting for transfers between devices: 17.9 us -> 19.8 us
  Pallas kernels: 36.5 us -> 34.9 us
    all_to_all x1 -> x0, blocking collectives: 20.6 us -> none  [z_exchange(): lax.all_to_all(x, 'seq', 0, 0, axis_index_groups=SAME_CORE, tiled=True)]
    ppermute x7 -> x9, starting transfers between devices: 12.9 us -> 17 us  [the longest x6 9.4 us: y_send(): return lax.ppermute(x, 'cam', moves)]
    all_to_all x1 -> x0, starting transfers between devices: 3.98 us -> none  [cam_exchange(): return lax.all_to_all(x, 'cam', 0, 0, tiled=True)]
    all_to_all x1 -> x2, starting transfers between devices: 10 us -> 13.9 us  [z_exchange(): lax.all_to_all(x, 'seq', 0, 0, axis_index_groups=SAME_CORE, tiled=True)]
    all_to_all x1 -> x2, waiting for transfers between devices: 0.01 us -> 3.36 us  [z_exchange(): lax.all_to_all(x, 'seq', 0, 0, axis_index_groups=SAME_CORE, tiled=True)]
    unnamed x19 -> x27, local copies, waits for them, and re-layouts: 1.38 us -> 4.04 us
    ppermute x1, starting transfers between devices: 6.97 us -> 5.05 us  [shards(): other = lax.ppermute(mine, 'seq', [(s, s ^ 1) for s in range(4 * NZ)])]
    ppermute x7 -> x9, waiting for transfers between devices: 17.9 us -> 16 us  [the longest x1 6.85 us: shards(): lax.ppermute(strip_kv[0, 1], 'cam', [(c, (c + 1) % CAMS) for c in ring])]
  transfers between devices with their start and end apart: 10 -> 12, of which waited for: 3 -> 7; matrix products, arithmetic and copies ran while one was open for 1% -> 2% of each run, Pallas kernels for 28% -> 30%
where the time goes in v2:
time: 97.7 us; the launch traced here: 97.3 us
  starting transfers between devices  36 us (37%)
  Pallas kernels  34.9 us (36%)
  waiting for transfers between devices  19.8 us (20%)
  local copies, waits for them, and re-layouts  5.09 us (5%)
  between operations  1.43 us (1%)
    pallas_call x1, Pallas kernels, shards(): pl.pallas_call(self_kernel, out_shape=of((PLACES, O_ROWS, LANES)), scratc...  17.2 us
    all_to_all x2, starting transfers between devices, z_exchange(): lax.all_to_all(x, 'seq', 0, 0, axis_index_groups=SAME_CORE, tiled=True)  13.9 us
    ppermute x6, starting transfers between devices, y_send(): return lax.ppermute(x, 'cam', moves)  9.4 us
    ppermute x1, waiting for transfers between devices, shards(): lax.ppermute(strip_kv[0, 1], 'cam', [(c, (c + 1) % CAMS) for c in ring])  6.85 us
    ppermute x6, waiting for transfers between devices, y_send(): return lax.ppermute(x, 'cam', moves)  6.66 us
    pallas_call x1, Pallas kernels, shards(): pl.pallas_call(layout_kernel, out_shape=[of((TOK, GROUP_COLS))] * NY, scr...  5.84 us
    ppermute x1, starting transfers between devices, shards(): other = lax.ppermute(mine, 'seq', [(s, s ^ 1) for s in range(4 * NZ)])  5.05 us
    ppermute x1, starting transfers between devices, shards(): lax.ppermute(strip_kv[0, 0], 'cam', [(c, (c - 1) % CAMS) for c in ring])  4.68 us
  transfers between devices with their start and end apart: 12, of which 7 were waited for; matrix products, arithmetic and copies ran while one was open for 2% of the time, Pallas kernels for 30%

profile of v2, /device:TPU:1, one launch (start us, length us, event | category | flops | bytes accessed | tf_op | source)
XLA Modules:
  0.0 97.3 jit_solution(10409315018770055909)
XLA Ops:
  0.0 2.8 %pack_z.1 = bf16[16,352,128]{2,1,0:T(8,128)(2,1)} custom-call(bf16[128,1536]{1,0:T(8,128)(2,1)} %bitcast.15, bf16[128,1536]{1,0:T(8,128)(2,1)} %bitcast.18, bf16[128,1536]{1,0:T(8,128)(2,1)} %bitcast.19), custom_call_target="tpu_custom_call" | custom-call | bytes 2359296 | tf_op jit(solution)/shard_map/pack_z/pallas_call | solution.py:283
  2.8 10.2 %all-to-all-start = ((bf16[16,352,128]{2,1,0:T(8,128)(2,1)}), bf16[16,352,128]{2,1,0:T(8,128)(2,1)S(1)}, u32[]{:S(2)}, u32[]{:S(2)}) async-start(bf16[16,352,128]{2,1,0:T(8,128)(2,1)} %pack_z.1), calls=%async_computation | async-start | bytes 2883584 | tf_op jit(solution)/shard_map/all_to_all | solution.py:268
  13.6 2.4 %pack_cam.1 = (bf16[400,384]{1,0:T(8,128)(2,1)}, bf16[400,384]{1,0:T(8,128)(2,1)}, bf16[400,384]{1,0:T(8,128)(2,1)}, bf16[400,384]{1,0:T(8,128)(2,1)}) custom-call(s32[1,1,3]{2,1,0:T(1,128)} %list_ref.1, s32[1,1]{1,0:T(1,128)S(6)} %copy.14.count_ref, bf16[128,1536]{1,0:T(8,128)(2,1)} %bitcast.16, bf16[128,1536]{1,0:T(8,128)(2,1)} %k_ref.1, ...), custom_call_target="tpu_custom_call" | custom-call | bytes 2359296 | tf_op jit(solution)/shard_map/pack_cam/pallas_call | solution.py:291
  16.0 1.3 %collective-permute-start.2 = (bf16[400,384]{1,0:T(8,128)(2,1)}, bf16[400,384]{1,0:T(8,128)(2,1)S(1)}, u32[]{:S(2)}, u32[]{:S(2)}) collective-permute-start(bf16[400,384]{1,0:T(8,128)(2,1)} %get-tuple-element.16), channel_id=1, source_target_pairs={{0,32},{32,64},{64,96},{96,0},{128,160},{160,192},{192,224},{224,1... | collective-permute-start | bytes 921608 | tf_op jit(solution)/shard_map/ppermute | solution.py:273
  17.3 2.6 %collective-permute-start.3 = (bf16[400,384]{1,0:T(8,128)(2,1)}, bf16[400,384]{1,0:T(8,128)(2,1)S(1)}, u32[]{:S(2)}, u32[]{:S(2)}) collective-permute-start(bf16[400,384]{1,0:T(8,128)(2,1)} %get-tuple-element.17), channel_id=1, source_target_pairs={{0,64},{32,96},{64,0},{96,32},{128,192},{160,224},{192,128},{224,1... | collective-permute-start | bytes 921608 | tf_op jit(solution)/shard_map/ppermute | solution.py:273
  19.9 1.1 %collective-permute-start.4 = (bf16[400,384]{1,0:T(8,128)(2,1)}, bf16[400,384]{1,0:T(8,128)(2,1)S(1)}, u32[]{:S(2)}, u32[]{:S(2)}) collective-permute-start(bf16[400,384]{1,0:T(8,128)(2,1)} %get-tuple-element.18), channel_id=1, source_target_pairs={{0,96},{32,0},{64,32},{96,64},{128,224},{160,128},{192,160},{224,1... | collective-permute-start | bytes 921608 | tf_op jit(solution)/shard_map/ppermute | solution.py:273
  21.5 4.7 %collective-permute-start.1 = (bf16[2,32,1536]{2,1,0:T(8,128)(2,1)S(1)}, bf16[2,32,1536]{2,1,0:T(8,128)(2,1)S(1)}, u32[]{:S(2)}, u32[]{:S(2)}) collective-permute-start(bf16[2,32,1536]{2,1,0:T(8,128)(2,1)S(1)} %get-tuple-element.25), channel_id=1, source_target_pairs={{0,224},{32,0},{64,32},{96,64},{128,96},{160,128},{192,160},{224,1... | collective-permute-start | bytes 589832 | tf_op jit(solution)/shard_map/ppermute | solution.py:302
  26.2 0.9 slice.20
  27.2 6.8 %collective-permute-done.left_ref = bf16[2,32,1536]{2,1,0:T(8,128)(2,1)S(1)} collective-permute-done((bf16[2,32,1536]{2,1,0:T(8,128)(2,1)S(1)}, bf16[2,32,1536]{2,1,0:T(8,128)(2,1)S(1)}, u32[]{:S(2)}, u32[]{:S(2)}) %collective-permute-start) | collective-permute-done | bytes 196640 | tf_op jit(solution)/shard_map/ppermute | solution.py:301
  34.0 2.5 %collective-permute-done.1.right_ref = bf16[2,32,1536]{2,1,0:T(8,128)(2,1)S(1)} collective-permute-done((bf16[2,32,1536]{2,1,0:T(8,128)(2,1)S(1)}, bf16[2,32,1536]{2,1,0:T(8,128)(2,1)S(1)}, u32[]{:S(2)}, u32[]{:S(2)}) %collective-permute-start.1) | collective-permute-done | bytes 196640 | tf_op jit(solution)/shard_map/ppermute | solution.py:302
  36.5 0.7 copy-done.5
  37.2 4.2 %view_attention.1.refs_4_ = f32[128,1536]{1,0:T(8,128)} custom-call(bf16[128,1536]{1,0:T(8,128)(2,1)} %bitcast.17, bf16[2,32,1536]{2,1,0:T(8,128)(2,1)} %copy-done.4, bf16[2,32,1536]{2,1,0:T(8,128)(2,1)} %copy-done.5), custom_call_target="tpu_custom_call" | custom-call | flops 201326592 | bytes 786432 | tf_op jit(solution)/shard_map/view_attention/pallas_call | solution.py:303
  42.4 3.4 %all-to-all-done.mine_ref = bf16[16,352,128]{2,1,0:T(8,128)(2,1)S(1)} async-done(((bf16[16,352,128]{2,1,0:T(8,128)(2,1)}), bf16[16,352,128]{2,1,0:T(8,128)(2,1)S(1)}, u32[]{:S(2)}, u32[]{:S(2)}) %all-to-all-start) | async-done | bytes 1441824 | tf_op jit(solution)/shard_map/all_to_all | solution.py:268
  45.8 5.1 %collective-permute-start.5 = (bf16[16,352,128]{2,1,0:T(8,128)(2,1)S(1)}, bf16[16,352,128]{2,1,0:T(8,128)(2,1)S(1)}, u32[]{:S(2)}, u32[]{:S(2)}) collective-permute-start(bf16[16,352,128]{2,1,0:T(8,128)(2,1)S(1)} %all-to-all-done.mine_ref), channel_id=1, source_target_pairs={{0,1},{1,0},{2,3},{3,2},{4,5},{5,4},{6,7},{7,6},{8,9},{9,8},{10,11... | collective-permute-start | bytes 4325384 | tf_op jit(solution)/shard_map/ppermute | solution.py:313
  50.8 2.5 %collective-permute-start.6 = (bf16[1024,384]{1,0:T(8,128)(2,1)S(1)}, bf16[1024,384]{1,0:T(8,128)(2,1)}, u32[]{:S(2)}, u32[]{:S(2)}) collective-permute-start(bf16[1024,384]{1,0:T(8,128)(2,1)S(1)} %pad_maximum_fusion), channel_id=1, source_target_pairs={{0,128},{32,160},{64,192},{96,224},{128,0},{160,32},{192,64},{224,... | collective-permute-start | bytes 2359304 | tf_op jit(solution)/shard_map/ppermute | solution.py:311
  53.7 1.1 %copy-done.12 = bf16[16,352,128]{2,1,0:T(8,128)(2,1)} copy-done((bf16[16,352,128]{2,1,0:T(8,128)(2,1)}, bf16[16,352,128]{2,1,0:T(8,128)(2,1)S(1)}, u32[]{:S(2)}) %copy-start.12) | copy-done | bytes 1441816
  54.8 17.2 %self_attention.1 = bf16[16,96,128]{2,1,0:T(8,128)(2,1)} custom-call(bf16[16,352,128]{2,1,0:T(8,128)(2,1)} %copy-done.2, bf16[16,352,128]{2,1,0:T(8,128)(2,1)} %copy-done.12), custom_call_target="tpu_custom_call" | custom-call | flops 12884901888 | bytes 4194304 | tf_op jit(solution)/shard_map/self_attention/pallas_call | solution.py:315
  72.0 3.7 %all-to-all-start.1 = ((bf16[16,96,128]{2,1,0:T(8,128)(2,1)}), bf16[16,96,128]{2,1,0:T(8,128)(2,1)S(1)}, u32[]{:S(2)}, u32[]{:S(2)}) async-start(bf16[16,96,128]{2,1,0:T(8,128)(2,1)} %self_attention.1), calls=%async_computation.1 | async-start | bytes 786432 | tf_op jit(solution)/shard_map/all_to_all | solution.py:268
  76.4 5.8 %layout_attention.1 = (bf16[128,384]{1,0:T(8,128)(2,1)}, bf16[128,384]{1,0:T(8,128)(2,1)}, bf16[128,384]{1,0:T(8,128)(2,1)}, bf16[128,384]{1,0:T(8,128)(2,1)}) custom-call(bf16[400,384]{1,0:T(8,128)(2,1)} %get-tuple-element.15.refs_0_, bf16[400,384]{1,0:T(8,128)(2,1)} %copy-done.6, bf16[400,384]{1,0:T(8,128)(2,1)} %copy-done.7, bf16[400,384]{1,0:T(8,128)(2,1)} %copy-done.8, ...), custom_call_target="tpu_custom_call" | custom-call | flops 1207959552 | bytes 786432 | tf_op jit(solution)/shard_map/layout_attention/pallas_call | solution.py:331
  82.3 3.8 %collective-permute-start.7 = (bf16[128,384]{1,0:T(8,128)(2,1)}, bf16[128,384]{1,0:T(8,128)(2,1)S(1)}, u32[]{:S(2)}, u32[]{:S(2)}) collective-permute-start(bf16[128,384]{1,0:T(8,128)(2,1)} %get-tuple-element.22), channel_id=1, source_target_pairs={{0,96},{32,0},{64,32},{96,64},{128,224},{160,128},{192,160},{224,1... | collective-permute-start | bytes 294920 | tf_op jit(solution)/shard_map/ppermute | solution.py:273
  87.3 3.3 %collective-permute-done.7.refs_1_ = bf16[128,384]{1,0:T(8,128)(2,1)S(1)} collective-permute-done((bf16[128,384]{1,0:T(8,128)(2,1)}, bf16[128,384]{1,0:T(8,128)(2,1)S(1)}, u32[]{:S(2)}, u32[]{:S(2)}) %collective-permute-start.7) | collective-permute-done | bytes 98336 | tf_op jit(solution)/shard_map/ppermute | solution.py:273
  90.6 0.8 collective-permute-done.8.refs_2_
  91.4 2.6 %collective-permute-done.9.refs_3_ = bf16[128,384]{1,0:T(8,128)(2,1)S(1)} collective-permute-done((bf16[128,384]{1,0:T(8,128)(2,1)}, bf16[128,384]{1,0:T(8,128)(2,1)S(1)}, u32[]{:S(2)}, u32[]{:S(2)}) %collective-permute-start.9) | collective-permute-done | bytes 98336 | tf_op jit(solution)/shard_map/ppermute | solution.py:273
  94.8 2.5 %blend.1 = bf16[128,1536]{1,0:T(8,128)(2,1)} custom-call(bf16[16,96,128]{2,1,0:T(8,128)(2,1)} %copy-done.1, bf16[128,384]{1,0:T(8,128)(2,1)} %get-tuple-element.21.refs_0_, bf16[128,384]{1,0:T(8,128)(2,1)} %copy-done.9, bf16[128,384]{1,0:T(8,128)(2,1)} %copy-done.10, bf16[128,384]{1,0:T(8,128)(2,1)} %copy-done.11, f32[128,1536]{1,0:T(8,128)} %view_attention.1.refs_4_, ...), custom_call_target="tpu_custom_call" | custom-call | bytes 1966080 | tf_op jit(solution)/shard_map/blend/pallas_call | solution.py:344
  (40 shorter events, 3.9 us)
Async XLA Ops:
  0.0 86.7 %copy-start = (f32[50,3,1536]{2,0,1:T(8,128)S(1)}, f32[50,3,1536]{2,0,1:T(8,128)}, u32[]{:S(2)}) copy-start(f32[50,3,1536]{2,0,1:T(8,128)} %param.18) | copy-start | bytes 2764804
  2.8 18.2 %copy-start.3 = (bf16[1,2,2,32,1536]{4,3,2,1,0:T(8,128)(2,1)S(1)}, bf16[1,2,2,32,1536]{4,3,2,1,0:T(8,128)(2,1)}, u32[]{:S(2)}) copy-start(bf16[1,2,2,32,1536]{4,3,2,1,0:T(8,128)(2,1)} %param.13) | copy-start | bytes 1179652
  2.8 43.0 %all-to-all-start = ((bf16[16,352,128]{2,1,0:T(8,128)(2,1)}), bf16[16,352,128]{2,1,0:T(8,128)(2,1)S(1)}, u32[]{:S(2)}, u32[]{:S(2)}) async-start(bf16[16,352,128]{2,1,0:T(8,128)(2,1)} %pack_z.1), calls=%async_computation | async-start | bytes 2883584 | tf_op jit(solution)/shard_map/all_to_all | solution.py:268
  16.0 25.4 %collective-permute-start.2 = (bf16[400,384]{1,0:T(8,128)(2,1)}, bf16[400,384]{1,0:T(8,128)(2,1)S(1)}, u32[]{:S(2)}, u32[]{:S(2)}) collective-permute-start(bf16[400,384]{1,0:T(8,128)(2,1)} %get-tuple-element.16), channel_id=1, source_target_pairs={{0,32},{32,64},{64,96},{96,0},{128,160},{160,192},{192,224},{224,1... | collective-permute-start | bytes 921608 | tf_op jit(solution)/shard_map/ppermute | solution.py:273
  17.3 24.1 %collective-permute-start.3 = (bf16[400,384]{1,0:T(8,128)(2,1)}, bf16[400,384]{1,0:T(8,128)(2,1)S(1)}, u32[]{:S(2)}, u32[]{:S(2)}) collective-permute-start(bf16[400,384]{1,0:T(8,128)(2,1)} %get-tuple-element.17), channel_id=1, source_target_pairs={{0,64},{32,96},{64,0},{96,32},{128,192},{160,224},{192,128},{224,1... | collective-permute-start | bytes 921608 | tf_op jit(solution)/shard_map/ppermute | solution.py:273
  19.9 21.5 %collective-permute-start.4 = (bf16[400,384]{1,0:T(8,128)(2,1)}, bf16[400,384]{1,0:T(8,128)(2,1)S(1)}, u32[]{:S(2)}, u32[]{:S(2)}) collective-permute-start(bf16[400,384]{1,0:T(8,128)(2,1)} %get-tuple-element.18), channel_id=1, source_target_pairs={{0,96},{32,0},{64,32},{96,64},{128,224},{160,128},{192,160},{224,1... | collective-permute-start | bytes 921608 | tf_op jit(solution)/shard_map/ppermute | solution.py:273
  21.1 13.0 %collective-permute-start = (bf16[2,32,1536]{2,1,0:T(8,128)(2,1)S(1)}, bf16[2,32,1536]{2,1,0:T(8,128)(2,1)S(1)}, u32[]{:S(2)}, u32[]{:S(2)}) collective-permute-start(bf16[2,32,1536]{2,1,0:T(8,128)(2,1)S(1)} %get-tuple-element.26), channel_id=1, source_target_pairs={{0,32},{32,64},{64,96},{96,128},{128,160},{160,192},{192,224},{224... | collective-permute-start | bytes 589832 | tf_op jit(solution)/shard_map/ppermute | solution.py:301
  21.5 15.0 %collective-permute-start.1 = (bf16[2,32,1536]{2,1,0:T(8,128)(2,1)S(1)}, bf16[2,32,1536]{2,1,0:T(8,128)(2,1)S(1)}, u32[]{:S(2)}, u32[]{:S(2)}) collective-permute-start(bf16[2,32,1536]{2,1,0:T(8,128)(2,1)S(1)} %get-tuple-element.25), channel_id=1, source_target_pairs={{0,224},{32,0},{64,32},{96,64},{128,96},{160,128},{192,160},{224,1... | collective-permute-start | bytes 589832 | tf_op jit(solution)/shard_map/ppermute | solution.py:302
  34.0 2.5 %copy-start.4 = (bf16[2,32,1536]{2,1,0:T(8,128)(2,1)}, bf16[2,32,1536]{2,1,0:T(8,128)(2,1)S(1)}, u32[]{:S(2)}) copy-start(bf16[2,32,1536]{2,1,0:T(8,128)(2,1)S(1)} %collective-permute-done.left_ref) | copy-start | bytes 589828
  36.5 0.7 copy-start.5
  41.4 0.7 copy-start.6
  41.4 0.8 copy-start.7
  41.5 0.9 copy-start.8
  45.8 7.9 %copy-start.2 = (bf16[16,352,128]{2,1,0:T(8,128)(2,1)}, bf16[16,352,128]{2,1,0:T(8,128)(2,1)S(1)}, u32[]{:S(2)}) copy-start(bf16[16,352,128]{2,1,0:T(8,128)(2,1)S(1)} %all-to-all-done.mine_ref) | copy-start | bytes 4325380
  45.8 7.9 %collective-permute-start.5 = (bf16[16,352,128]{2,1,0:T(8,128)(2,1)S(1)}, bf16[16,352,128]{2,1,0:T(8,128)(2,1)S(1)}, u32[]{:S(2)}, u32[]{:S(2)}) collective-permute-start(bf16[16,352,128]{2,1,0:T(8,128)(2,1)S(1)} %all-to-all-done.mine_ref), channel_id=1, source_target_pairs={{0,1},{1,0},{2,3},{3,2},{4,5},{5,4},{6,7},{7,6},{8,9},{9,8},{10,11... | collective-permute-start | bytes 4325384 | tf_op jit(solution)/shard_map/ppermute | solution.py:313
  50.8 25.6 %collective-permute-start.6 = (bf16[1024,384]{1,0:T(8,128)(2,1)S(1)}, bf16[1024,384]{1,0:T(8,128)(2,1)}, u32[]{:S(2)}, u32[]{:S(2)}) collective-permute-start(bf16[1024,384]{1,0:T(8,128)(2,1)S(1)} %pad_maximum_fusion), channel_id=1, source_target_pairs={{0,128},{32,160},{64,192},{96,224},{128,0},{160,32},{192,64},{224,... | collective-permute-start | bytes 2359304 | tf_op jit(solution)/shard_map/ppermute | solution.py:311
  53.7 1.1 %copy-start.12 = (bf16[16,352,128]{2,1,0:T(8,128)(2,1)}, bf16[16,352,128]{2,1,0:T(8,128)(2,1)S(1)}, u32[]{:S(2)}) copy-start(bf16[16,352,128]{2,1,0:T(8,128)(2,1)S(1)} %collective-permute-done.5.other_ref) | copy-start | bytes 4325380
  72.0 22.0 %all-to-all-start.1 = ((bf16[16,96,128]{2,1,0:T(8,128)(2,1)}), bf16[16,96,128]{2,1,0:T(8,128)(2,1)S(1)}, u32[]{:S(2)}, u32[]{:S(2)}) async-start(bf16[16,96,128]{2,1,0:T(8,128)(2,1)} %self_attention.1), calls=%async_computation.1 | async-start | bytes 786432 | tf_op jit(solution)/shard_map/all_to_all | solution.py:268
  82.3 8.3 %collective-permute-start.7 = (bf16[128,384]{1,0:T(8,128)(2,1)}, bf16[128,384]{1,0:T(8,128)(2,1)S(1)}, u32[]{:S(2)}, u32[]{:S(2)}) collective-permute-start(bf16[128,384]{1,0:T(8,128)(2,1)} %get-tuple-element.22), channel_id=1, source_target_pairs={{0,96},{32,0},{64,32},{96,64},{128,224},{160,128},{192,160},{224,1... | collective-permute-start | bytes 294920 | tf_op jit(solution)/shard_map/ppermute | solution.py:273
  86.1 5.3 %collective-permute-start.8 = (bf16[128,384]{1,0:T(8,128)(2,1)}, bf16[128,384]{1,0:T(8,128)(2,1)S(1)}, u32[]{:S(2)}, u32[]{:S(2)}) collective-permute-start(bf16[128,384]{1,0:T(8,128)(2,1)} %get-tuple-element.23), channel_id=1, source_target_pairs={{0,64},{32,96},{64,0},{96,32},{128,192},{160,224},{192,128},{224,1... | collective-permute-start | bytes 294920 | tf_op jit(solution)/shard_map/ppermute | solution.py:273
  86.1 7.9 %collective-permute-start.9 = (bf16[128,384]{1,0:T(8,128)(2,1)}, bf16[128,384]{1,0:T(8,128)(2,1)S(1)}, u32[]{:S(2)}, u32[]{:S(2)}) collective-permute-start(bf16[128,384]{1,0:T(8,128)(2,1)} %get-tuple-element.24), channel_id=1, source_target_pairs={{0,32},{32,64},{64,96},{96,0},{128,160},{160,192},{192,224},{224,1... | collective-permute-start | bytes 294920 | tf_op jit(solution)/shard_map/ppermute | solution.py:273
  90.6 3.4 %copy-start.9 = (bf16[128,384]{1,0:T(8,128)(2,1)}, bf16[128,384]{1,0:T(8,128)(2,1)S(1)}, u32[]{:S(2)}) copy-start(bf16[128,384]{1,0:T(8,128)(2,1)S(1)} %collective-permute-done.7.refs_1_) | copy-start | bytes 294916
  91.4 2.6 %copy-start.10 = (bf16[128,384]{1,0:T(8,128)(2,1)}, bf16[128,384]{1,0:T(8,128)(2,1)S(1)}, u32[]{:S(2)}) copy-start(bf16[128,384]{1,0:T(8,128)(2,1)S(1)} %collective-permute-done.8.refs_2_) | copy-start | bytes 294916
  94.0 0.8 copy-start.1
  (1 other events, 0.6 us)

commit v3 on v2

--- a/solution.py
+++ b/solution.py
@@ -29,7 +29,7 @@
 V_ROWS = 80
 SCALE = math.log2(math.e) / math.sqrt(HALF)
 NT = (((1,), (1,)), ((), ()))
-VMEM_LIMIT = 56 * 2**20
+MIB = 2**20
 
 Q_ONE = TOK
 KV_TWO = Q_ONE + TOK // 2
@@ -66,11 +66,17 @@
     return ref[:, index * LANES : (index + 1) * LANES]
 
 
-def params():
-    return pltpu.CompilerParams(vmem_limit_bytes=VMEM_LIMIT)
-
-
-def pack_z_kernel(q_ref, k_ref, v_ref, out_ref):
+def params(mib=12):
+    return pltpu.CompilerParams(vmem_limit_bytes=mib * MIB)
+
+
+def pack_z_kernel(q_hbm, k_hbm, v_hbm, out_ref, q_ref, k_ref, v_ref, sems):
+    pairs = ((k_hbm, k_ref), (v_hbm, v_ref), (q_hbm, q_ref))
+    copies = [pltpu.make_async_copy(a, b, sems.at[i]) for i, (a, b) in enumerate(pairs)]
+    for copy in copies:
+        copy.start()
+    for copy in copies:
+        copy.wait()
     for z in range(NZ):
         at, half = NZ + z // 2, z % 2
         shared = side_by_side(tile(k_ref, at), half, tile(v_ref, at), half)
@@ -283,10 +289,12 @@
     to_z = pl.pallas_call(
         pack_z_kernel,
         out_shape=of((PLACES, Z_ROWS, LANES)),
+        in_specs=[pl.BlockSpec(memory_space=pltpu.HBM)] * 3,
+        scratch_shapes=[pltpu.VMEM((TOK, WIDTH), BF)] * 3 + [pltpu.SemaphoreType.DMA((3,))],
         compiler_params=params(),
         cost_estimate=cost(0, 2 * 6 * TOK * WIDTH, 0),
         name="pack_z",
-    )(q, k, v)
+    )(*(pltpu.with_memory_space_constraint(t, pltpu.HBM) for t in (q, k, v)))
     mine = z_exchange(to_z)
     to_cam = pl.pallas_call(
         pack_cam_kernel,
@@ -309,7 +317,7 @@
     )(q, from_left, from_right)
     to_far = jnp.concatenate([t[:C_Q] for t in got], axis=0)
     far = lax.ppermute(to_far, "cam", [(c, (c + NY) % CAMS) for c in ring])
-    mine = after(mine, view, to_far)
+    mine = after(mine, view, to_far, gains)
     other = lax.ppermute(mine, "seq", [(s, s ^ 1) for s in range(4 * NZ)])
     queries = 3 * NZ * TOK
     self_out = pl.pallas_call(
@@ -322,7 +330,7 @@
             pltpu.VMEM((2, 8, BQ), F32),
             pltpu.VMEM((queries, LANES), F32),
         ],
-        compiler_params=params(),
+        compiler_params=params(24),
         cost_estimate=cost(16 * queries * KEYS * HALF, 8 * KEYS * LANES, queries * KEYS),
         name="self_attention",
     )(mine, other)

time: 97.7 us -> 93.1 us (0.953)
  Pallas kernels: 34.9 us -> 30.4 us
  local copies, waits for them, and re-layouts: 5.09 us -> 1.78 us
  waiting for transfers between devices: 19.8 us -> 22.6 us
    unnamed x27 -> x15, local copies, waits for them, and re-layouts: 4.04 us -> 0.05 us
    all_to_all x2, waiting for transfers between devices: 3.36 us -> 5.95 us  [z_exchange(): lax.all_to_all(x, 'seq', 0, 0, axis_index_groups=SAME_CORE, tiled=True)]
    pallas_call x1, Pallas kernels: 4.17 us -> 2.11 us  [shards(): pl.pallas_call(view_kernel, out_shape=of((TOK, WIDTH), F32), compiler_par...]
    pallas_call x1, Pallas kernels: 2.49 us -> 1.13 us  [shards(): pl.pallas_call(blend_kernel, out_shape=of((TOK, WIDTH)), scratch_shapes=[...]
  transfers between devices with their start and end apart: 12 -> 12, of which waited for: 7 -> 7; matrix products, arithmetic and copies ran while one was open for 2% -> 3% of each run, Pallas kernels for 30% -> 28%
where the time goes in v3:
time: 93.1 us; the launch traced here: 92.8 us
  starting transfers between devices  35.5 us (38%)
  Pallas kernels  30.4 us (33%)
  waiting for transfers between devices  22.6 us (24%)
  local copies, waits for them, and re-layouts  1.78 us (2%)
  between operations  1.52 us (2%)
  other arithmetic  0.97 us (1%)
    pallas_call x1, Pallas kernels, shards(): pl.pallas_call(self_kernel, out_shape=of((PLACES, O_ROWS, LANES)), scratc...  17.8 us
    all_to_all x2, starting transfers between devices, z_exchange(): lax.all_to_all(x, 'seq', 0, 0, axis_index_groups=SAME_CORE, tiled=True)  14 us
    ppermute x6, starting transfers between devices, y_send(): return lax.ppermute(x, 'cam', moves)  8.84 us
    ppermute x6, waiting for transfers between devices, y_send(): return lax.ppermute(x, 'cam', moves)  7.16 us
    ppermute x1, waiting for transfers between devices, shards(): lax.ppermute(strip_kv[0, 1], 'cam', [(c, (c + 1) % CAMS) for c in ring])  6.39 us
    all_to_all x2, waiting for transfers between devices, z_exchange(): lax.all_to_all(x, 'seq', 0, 0, axis_index_groups=SAME_CORE, tiled=True)  5.95 us
    ppermute x1, starting transfers between devices, shards(): other = lax.ppermute(mine, 'seq', [(s, s ^ 1) for s in range(4 * NZ)])  5.05 us
    pallas_call x1, Pallas kernels, shards(): pl.pallas_call(layout_kernel, out_shape=[of((TOK, GROUP_COLS))] * NY, scr...  4.96 us
  transfers between devices with their start and end apart: 12, of which 7 were waited for; matrix products, arithmetic and copies ran while one was open for 3% of the time, Pallas kernels for 28%

profile of v3, /device:TPU:1, one launch (start us, length us, event | category | flops | bytes accessed | tf_op | source)
XLA Modules:
  0.0 92.8 jit_solution(8981792143299307108)
XLA Ops:
  0.0 2.8 %pack_z.1 = bf16[16,352,128]{2,1,0:T(8,128)(2,1)} custom-call(bf16[128,1536]{1,0:T(8,128)(2,1)} %bitcast.15, bf16[128,1536]{1,0:T(8,128)(2,1)} %bitcast.19, bf16[128,1536]{1,0:T(8,128)(2,1)} %bitcast.20), custom_call_target="tpu_custom_call" | custom-call | bytes 2359296 | tf_op jit(solution)/shard_map/pack_z/pallas_call | solution.py:289
  2.9 10.2 %all-to-all-start = ((bf16[16,352,128]{2,1,0:T(8,128)(2,1)}), bf16[16,352,128]{2,1,0:T(8,128)(2,1)}, u32[]{:S(2)}, u32[]{:S(2)}) async-start(bf16[16,352,128]{2,1,0:T(8,128)(2,1)} %pack_z.1), calls=%async_computation | async-start | bytes 2883584 | tf_op jit(solution)/shard_map/all_to_all | solution.py:274
  13.8 1.6 %pack_cam.1 = (bf16[400,384]{1,0:T(8,128)(2,1)S(1)}, bf16[400,384]{1,0:T(8,128)(2,1)}, bf16[400,384]{1,0:T(8,128)(2,1)}, bf16[400,384]{1,0:T(8,128)(2,1)}) custom-call(s32[1,1,3]{2,1,0:T(1,128)S(1)} %copy-done.4, s32[1,1]{1,0:T(1,128)S(6)} %copy.14.count_ref, bf16[128,1536]{1,0:T(8,128)(2,1)S(1)} %bitcast.16, bf16[128,1536]{1,0:T(8,128)(2,1)S(1)} %copy-done.2, ...), custom_call_target="tpu_custom_call" | custom-call | bytes 2359296 | tf_op jit(solution)/shard_map/pack_cam/pallas_call | solution.py:299
  15.4 1.3 %collective-permute-start.2 = (bf16[400,384]{1,0:T(8,128)(2,1)}, bf16[400,384]{1,0:T(8,128)(2,1)S(1)}, u32[]{:S(2)}, u32[]{:S(2)}) collective-permute-start(bf16[400,384]{1,0:T(8,128)(2,1)} %get-tuple-element.16), channel_id=1, source_target_pairs={{0,32},{32,64},{64,96},{96,0},{128,160},{160,192},{192,224},{224,1... | collective-permute-start | bytes 921608 | tf_op jit(solution)/shard_map/ppermute | solution.py:279
  16.7 2.6 %collective-permute-start.3 = (bf16[400,384]{1,0:T(8,128)(2,1)}, bf16[400,384]{1,0:T(8,128)(2,1)S(1)}, u32[]{:S(2)}, u32[]{:S(2)}) collective-permute-start(bf16[400,384]{1,0:T(8,128)(2,1)} %get-tuple-element.17), channel_id=1, source_target_pairs={{0,64},{32,96},{64,0},{96,32},{128,192},{160,224},{192,128},{224,1... | collective-permute-start | bytes 921608 | tf_op jit(solution)/shard_map/ppermute | solution.py:279
  19.3 1.1 %collective-permute-start.4 = (bf16[400,384]{1,0:T(8,128)(2,1)}, bf16[400,384]{1,0:T(8,128)(2,1)}, u32[]{:S(2)}, u32[]{:S(2)}) collective-permute-start(bf16[400,384]{1,0:T(8,128)(2,1)} %get-tuple-element.18), channel_id=1, source_target_pairs={{0,96},{32,0},{64,32},{96,64},{128,224},{160,128},{192,160},{224,1... | collective-permute-start | bytes 921608 | tf_op jit(solution)/shard_map/ppermute | solution.py:279
  20.9 4.7 %collective-permute-start.1 = (bf16[2,32,1536]{2,1,0:T(8,128)(2,1)S(1)}, bf16[2,32,1536]{2,1,0:T(8,128)(2,1)S(1)}, u32[]{:S(2)}, u32[]{:S(2)}) collective-permute-start(bf16[2,32,1536]{2,1,0:T(8,128)(2,1)S(1)} %get-tuple-element.25), channel_id=1, source_target_pairs={{0,224},{32,0},{64,32},{96,64},{128,96},{160,128},{192,160},{224,1... | collective-permute-start | bytes 589832 | tf_op jit(solution)/shard_map/ppermute | solution.py:310
  27.0 6.4 %collective-permute-done.left_ref = bf16[2,32,1536]{2,1,0:T(8,128)(2,1)S(1)} collective-permute-done((bf16[2,32,1536]{2,1,0:T(8,128)(2,1)S(1)}, bf16[2,32,1536]{2,1,0:T(8,128)(2,1)S(1)}, u32[]{:S(2)}, u32[]{:S(2)}) %collective-permute-start) | collective-permute-done | bytes 196640 | tf_op jit(solution)/shard_map/ppermute | solution.py:309
  33.4 2.5 %collective-permute-done.1.right_ref = bf16[2,32,1536]{2,1,0:T(8,128)(2,1)S(1)} collective-permute-done((bf16[2,32,1536]{2,1,0:T(8,128)(2,1)S(1)}, bf16[2,32,1536]{2,1,0:T(8,128)(2,1)S(1)}, u32[]{:S(2)}, u32[]{:S(2)}) %collective-permute-start.1) | collective-permute-done | bytes 196640 | tf_op jit(solution)/shard_map/ppermute | solution.py:310
  35.9 2.1 %view_attention.1.refs_4_ = f32[128,1536]{1,0:T(8,128)S(1)} custom-call(bf16[128,1536]{1,0:T(8,128)(2,1)S(1)} %bitcast.17, bf16[2,32,1536]{2,1,0:T(8,128)(2,1)S(1)} %collective-permute-done.left_ref, bf16[2,32,1536]{2,1,0:T(8,128)(2,1)S(1)} %collective-permute-done.1.right_ref), custom_call_target="tpu_custom_call" | custom-call | flops 201326592 | bytes 786432 | tf_op jit(solution)/shard_map/view_attention/pallas_call | solution.py:311
  38.1 0.9 %slice.26 = bf16[256,384]{1,0:T(8,128)(2,1)S(1)} slice(bf16[400,384]{1,0:T(8,128)(2,1)} %collective-permute-done.4.refs_3_), slice={[0:256], [0:384]} | slice | bytes 393216 | tf_op jit(solution)/shard_map/slice | solution.py:318
  39.1 1.0 %pad_maximum_fusion = bf16[1024,384]{1,0:T(8,128)(2,1)} fusion(bf16[256,384]{1,0:T(8,128)(2,1)S(1)} %slice.26, bf16[256,384]{1,0:T(8,128)(2,1)S(1)} %slice.25, bf16[256,384]{1,0:T(8,128)(2,1)S(1)} %slice.24, bf16[256,384]{1,0:T(8,128)(2,1)S(1)} %copy-done.5), kind=kLoop, calls=%fused_computation | loop fusion | flops 3145728 | bytes 1572864 | tf_op jit(solution)/shard_map/concatenate | solution.py:318
  40.0 5.9 %all-to-all-done.mine_ref = bf16[16,352,128]{2,1,0:T(8,128)(2,1)} async-done(((bf16[16,352,128]{2,1,0:T(8,128)(2,1)}), bf16[16,352,128]{2,1,0:T(8,128)(2,1)}, u32[]{:S(2)}, u32[]{:S(2)}) %all-to-all-start) | async-done | bytes 1441824 | tf_op jit(solution)/shard_map/all_to_all | solution.py:274
  46.0 5.1 %collective-permute-start.5 = (bf16[16,352,128]{2,1,0:T(8,128)(2,1)}, bf16[16,352,128]{2,1,0:T(8,128)(2,1)S(1)}, u32[]{:S(2)}, u32[]{:S(2)}) collective-permute-start(bf16[16,352,128]{2,1,0:T(8,128)(2,1)} %all-to-all-done.mine_ref), channel_id=1, source_target_pairs={{0,1},{1,0},{2,3},{3,2},{4,5},{5,4},{6,7},{7,6},{8,9},{9,8},{10,11... | collective-permute-start | bytes 4325384 | tf_op jit(solution)/shard_map/ppermute | solution.py:321
  51.0 2.5 %collective-permute-start.6 = (bf16[1024,384]{1,0:T(8,128)(2,1)}, bf16[1024,384]{1,0:T(8,128)(2,1)}, u32[]{:S(2)}, u32[]{:S(2)}) collective-permute-start(bf16[1024,384]{1,0:T(8,128)(2,1)} %pad_maximum_fusion), channel_id=1, source_target_pairs={{0,128},{32,160},{64,192},{96,224},{128,0},{160,32},{192,64},{224,... | collective-permute-start | bytes 2359304 | tf_op jit(solution)/shard_map/ppermute | solution.py:319
  54.1 17.8 %self_attention.1 = bf16[16,96,128]{2,1,0:T(8,128)(2,1)} custom-call(bf16[16,352,128]{2,1,0:T(8,128)(2,1)} %all-to-all-done.mine_ref, bf16[16,352,128]{2,1,0:T(8,128)(2,1)S(1)} %collective-permute-done.5.other_ref), custom_call_target="tpu_custom_call" | custom-call | flops 12884901888 | bytes 4194304 | tf_op jit(solution)/shard_map/self_attention/pallas_call | solution.py:323
  71.9 3.7 %all-to-all-start.1 = ((bf16[16,96,128]{2,1,0:T(8,128)(2,1)}), bf16[16,96,128]{2,1,0:T(8,128)(2,1)S(1)}, u32[]{:S(2)}, u32[]{:S(2)}) async-start(bf16[16,96,128]{2,1,0:T(8,128)(2,1)} %self_attention.1), calls=%async_computation.1 | async-start | bytes 786432 | tf_op jit(solution)/shard_map/all_to_all | solution.py:274
  75.7 5.0 %layout_attention.1 = (bf16[128,384]{1,0:T(8,128)(2,1)S(1)}, bf16[128,384]{1,0:T(8,128)(2,1)S(1)}, bf16[128,384]{1,0:T(8,128)(2,1)S(1)}, bf16[128,384]{1,0:T(8,128)(2,1)S(1)}) custom-call(bf16[400,384]{1,0:T(8,128)(2,1)S(1)} %get-tuple-element.15.refs_0_, bf16[400,384]{1,0:T(8,128)(2,1)S(1)} %collective-permute-done.2.refs_1_, ...), custom_call_target="tpu_custom_call" | custom-call | flops 1207959552 | bytes 786432 | tf_op jit(solution)/shard_map/layout_attention/pallas_call | solution.py:339
  80.6 2.8 %collective-permute-start.7 = (bf16[128,384]{1,0:T(8,128)(2,1)S(1)}, bf16[128,384]{1,0:T(8,128)(2,1)S(1)}, u32[]{:S(2)}, u32[]{:S(2)}) collective-permute-start(bf16[128,384]{1,0:T(8,128)(2,1)S(1)} %get-tuple-element.22), channel_id=1, source_target_pairs={{0,96},{32,0},{64,32},{96,64},{128,224},{160,128},{192,160},{224,1... | collective-permute-start | bytes 294920 | tf_op jit(solution)/shard_map/ppermute | solution.py:279
  83.8 0.7 collective-permute-start.9
  84.5 2.7 %collective-permute-done.7.refs_1_ = bf16[128,384]{1,0:T(8,128)(2,1)S(1)} collective-permute-done((bf16[128,384]{1,0:T(8,128)(2,1)S(1)}, bf16[128,384]{1,0:T(8,128)(2,1)S(1)}, u32[]{:S(2)}, u32[]{:S(2)}) %collective-permute-start.7) | collective-permute-done | bytes 98336 | tf_op jit(solution)/shard_map/ppermute | solution.py:279
  87.2 1.3 %collective-permute-done.8.refs_2_ = bf16[128,384]{1,0:T(8,128)(2,1)S(1)} collective-permute-done((bf16[128,384]{1,0:T(8,128)(2,1)S(1)}, bf16[128,384]{1,0:T(8,128)(2,1)S(1)}, u32[]{:S(2)}, u32[]{:S(2)}) %collective-permute-start.8) | collective-permute-done | bytes 98336 | tf_op jit(solution)/shard_map/ppermute | solution.py:279
  88.5 3.1 %collective-permute-done.9.refs_3_ = bf16[128,384]{1,0:T(8,128)(2,1)S(1)} collective-permute-done((bf16[128,384]{1,0:T(8,128)(2,1)S(1)}, bf16[128,384]{1,0:T(8,128)(2,1)S(1)}, u32[]{:S(2)}, u32[]{:S(2)}) %collective-permute-start.9) | collective-permute-done | bytes 98336 | tf_op jit(solution)/shard_map/ppermute | solution.py:279
  91.6 1.1 %blend.1 = bf16[128,1536]{1,0:T(8,128)(2,1)} custom-call(bf16[16,96,128]{2,1,0:T(8,128)(2,1)S(1)} %all-to-all-done.1.self_ref, bf16[128,384]{1,0:T(8,128)(2,1)S(1)} %get-tuple-element.21.refs_0_, bf16[128,384]{1,0:T(8,128)(2,1)S(1)} %collective-permute-done.7.refs_1_, bf16[128,384]{1,0:T(8,128)(2,1)S(1)} %collective-permute-done.8.refs_2_, ...), custom_call_target="tpu_custom_call" | custom-call | bytes 1966080 | tf_op jit(solution)/shard_map/blend/pallas_call | solution.py:352
  (28 shorter events, 2.3 us)
Async XLA Ops:
  0.0 26.9 %copy-start = (f32[50,3,1536]{2,0,1:T(8,128)S(1)}, f32[50,3,1536]{2,0,1:T(8,128)}, u32[]{:S(2)}) copy-start(f32[50,3,1536]{2,0,1:T(8,128)} %param.18) | copy-start | bytes 2764804
  2.8 11.0 %copy-start.1 = (bf16[1,128,1536]{2,1,0:T(8,128)(2,1)S(1)}, bf16[1,128,1536]{2,1,0:T(8,128)(2,1)}, u32[]{:S(2)}) copy-start(bf16[1,128,1536]{2,1,0:T(8,128)(2,1)} %param.10) | copy-start | bytes 1179652
  2.9 10.9 %copy-start.2 = (bf16[128,1536]{1,0:T(8,128)(2,1)S(1)}, bf16[128,1536]{1,0:T(8,128)(2,1)}, u32[]{:S(2)}) copy-start(bf16[128,1536]{1,0:T(8,128)(2,1)} %k_ref.1) | copy-start | bytes 1179652
  2.9 10.9 %copy-start.3 = (bf16[128,1536]{1,0:T(8,128)(2,1)S(1)}, bf16[128,1536]{1,0:T(8,128)(2,1)}, u32[]{:S(2)}) copy-start(bf16[128,1536]{1,0:T(8,128)(2,1)} %v_ref.1) | copy-start | bytes 1179652
  2.9 10.9 %copy-start.4 = (s32[1,1,3]{2,1,0:T(1,128)S(1)}, s32[1,1,3]{2,1,0:T(1,128)}, u32[]{:S(2)}) copy-start(s32[1,1,3]{2,1,0:T(1,128)} %list_ref.1) | copy-start | bytes 40
  2.9 17.5 %copy-start.6 = (bf16[1,2,2,32,1536]{4,3,2,1,0:T(8,128)(2,1)S(1)}, bf16[1,2,2,32,1536]{4,3,2,1,0:T(8,128)(2,1)}, u32[]{:S(2)}) copy-start(bf16[1,2,2,32,1536]{4,3,2,1,0:T(8,128)(2,1)} %param.13) | copy-start | bytes 1179652
  2.9 43.1 %all-to-all-start = ((bf16[16,352,128]{2,1,0:T(8,128)(2,1)}), bf16[16,352,128]{2,1,0:T(8,128)(2,1)}, u32[]{:S(2)}, u32[]{:S(2)}) async-start(bf16[16,352,128]{2,1,0:T(8,128)(2,1)} %pack_z.1), calls=%async_computation | async-start | bytes 2883584 | tf_op jit(solution)/shard_map/all_to_all | solution.py:274
  15.4 22.6 %collective-permute-start.2 = (bf16[400,384]{1,0:T(8,128)(2,1)}, bf16[400,384]{1,0:T(8,128)(2,1)S(1)}, u32[]{:S(2)}, u32[]{:S(2)}) collective-permute-start(bf16[400,384]{1,0:T(8,128)(2,1)} %get-tuple-element.16), channel_id=1, source_target_pairs={{0,32},{32,64},{64,96},{96,0},{128,160},{160,192},{192,224},{224,1... | collective-permute-start | bytes 921608 | tf_op jit(solution)/shard_map/ppermute | solution.py:279
  16.7 21.4 %collective-permute-start.3 = (bf16[400,384]{1,0:T(8,128)(2,1)}, bf16[400,384]{1,0:T(8,128)(2,1)S(1)}, u32[]{:S(2)}, u32[]{:S(2)}) collective-permute-start(bf16[400,384]{1,0:T(8,128)(2,1)} %get-tuple-element.17), channel_id=1, source_target_pairs={{0,64},{32,96},{64,0},{96,32},{128,192},{160,224},{192,128},{224,1... | collective-permute-start | bytes 921608 | tf_op jit(solution)/shard_map/ppermute | solution.py:279
  19.3 18.8 %collective-permute-start.4 = (bf16[400,384]{1,0:T(8,128)(2,1)}, bf16[400,384]{1,0:T(8,128)(2,1)}, u32[]{:S(2)}, u32[]{:S(2)}) collective-permute-start(bf16[400,384]{1,0:T(8,128)(2,1)} %get-tuple-element.18), channel_id=1, source_target_pairs={{0,96},{32,0},{64,32},{96,64},{128,224},{160,128},{192,160},{224,1... | collective-permute-start | bytes 921608 | tf_op jit(solution)/shard_map/ppermute | solution.py:279
  20.4 13.0 %collective-permute-start = (bf16[2,32,1536]{2,1,0:T(8,128)(2,1)S(1)}, bf16[2,32,1536]{2,1,0:T(8,128)(2,1)S(1)}, u32[]{:S(2)}, u32[]{:S(2)}) collective-permute-start(bf16[2,32,1536]{2,1,0:T(8,128)(2,1)S(1)} %get-tuple-element.26), channel_id=1, source_target_pairs={{0,32},{32,64},{64,96},{96,128},{128,160},{160,192},{192,224},{224... | collective-permute-start | bytes 589832 | tf_op jit(solution)/shard_map/ppermute | solution.py:309
  20.9 15.0 %collective-permute-start.1 = (bf16[2,32,1536]{2,1,0:T(8,128)(2,1)S(1)}, bf16[2,32,1536]{2,1,0:T(8,128)(2,1)S(1)}, u32[]{:S(2)}, u32[]{:S(2)}) collective-permute-start(bf16[2,32,1536]{2,1,0:T(8,128)(2,1)S(1)} %get-tuple-element.25), channel_id=1, source_target_pairs={{0,224},{32,0},{64,32},{96,64},{128,96},{160,128},{192,160},{224,1... | collective-permute-start | bytes 589832 | tf_op jit(solution)/shard_map/ppermute | solution.py:310
  26.9 12.1 %copy-start.5 = (bf16[256,384]{1,0:T(8,128)(2,1)S(1)}, bf16[256,384]{1,0:T(8,128)(2,1)}, u32[]{:S(2)}) copy-start(bf16[256,384]{1,0:T(8,128)(2,1)} %slice.20) | copy-start | bytes 589828
  46.0 8.1 %collective-permute-start.5 = (bf16[16,352,128]{2,1,0:T(8,128)(2,1)}, bf16[16,352,128]{2,1,0:T(8,128)(2,1)S(1)}, u32[]{:S(2)}, u32[]{:S(2)}) collective-permute-start(bf16[16,352,128]{2,1,0:T(8,128)(2,1)} %all-to-all-done.mine_ref), channel_id=1, source_target_pairs={{0,1},{1,0},{2,3},{3,2},{4,5},{5,4},{6,7},{7,6},{8,9},{9,8},{10,11... | collective-permute-start | bytes 4325384 | tf_op jit(solution)/shard_map/ppermute | solution.py:321
  51.0 24.6 %collective-permute-start.6 = (bf16[1024,384]{1,0:T(8,128)(2,1)}, bf16[1024,384]{1,0:T(8,128)(2,1)}, u32[]{:S(2)}, u32[]{:S(2)}) collective-permute-start(bf16[1024,384]{1,0:T(8,128)(2,1)} %pad_maximum_fusion), channel_id=1, source_target_pairs={{0,128},{32,160},{64,192},{96,224},{128,0},{160,32},{192,64},{224,... | collective-permute-start | bytes 2359304 | tf_op jit(solution)/shard_map/ppermute | solution.py:319
  71.9 19.7 %all-to-all-start.1 = ((bf16[16,96,128]{2,1,0:T(8,128)(2,1)}), bf16[16,96,128]{2,1,0:T(8,128)(2,1)S(1)}, u32[]{:S(2)}, u32[]{:S(2)}) async-start(bf16[16,96,128]{2,1,0:T(8,128)(2,1)} %self_attention.1), calls=%async_computation.1 | async-start | bytes 786432 | tf_op jit(solution)/shard_map/all_to_all | solution.py:274
  80.6 6.6 %collective-permute-start.7 = (bf16[128,384]{1,0:T(8,128)(2,1)S(1)}, bf16[128,384]{1,0:T(8,128)(2,1)S(1)}, u32[]{:S(2)}, u32[]{:S(2)}) collective-permute-start(bf16[128,384]{1,0:T(8,128)(2,1)S(1)} %get-tuple-element.22), channel_id=1, source_target_pairs={{0,96},{32,0},{64,32},{96,64},{128,224},{160,128},{192,160},{224,1... | collective-permute-start | bytes 294920 | tf_op jit(solution)/shard_map/ppermute | solution.py:279
  83.4 5.1 %collective-permute-start.8 = (bf16[128,384]{1,0:T(8,128)(2,1)S(1)}, bf16[128,384]{1,0:T(8,128)(2,1)S(1)}, u32[]{:S(2)}, u32[]{:S(2)}) collective-permute-start(bf16[128,384]{1,0:T(8,128)(2,1)S(1)} %get-tuple-element.23), channel_id=1, source_target_pairs={{0,64},{32,96},{64,0},{96,32},{128,192},{160,224},{192,128},{224,1... | collective-permute-start | bytes 294920 | tf_op jit(solution)/shard_map/ppermute | solution.py:279
  83.8 7.8 %collective-permute-start.9 = (bf16[128,384]{1,0:T(8,128)(2,1)S(1)}, bf16[128,384]{1,0:T(8,128)(2,1)S(1)}, u32[]{:S(2)}, u32[]{:S(2)}) collective-permute-start(bf16[128,384]{1,0:T(8,128)(2,1)S(1)} %get-tuple-element.24), channel_id=1, source_target_pairs={{0,32},{32,64},{64,96},{96,0},{128,160},{160,192},{192,224},{224,1... | collective-permute-start | bytes 294920 | tf_op jit(solution)/shard_map/ppermute | solution.py:279

commit v4 on v3

--- a/solution.py
+++ b/solution.py
@@ -105,14 +105,16 @@
         out_ref[C_META:] = uses
 
 
-def self_kernel(mine_ref, other_ref, o_ref, v_all, q_all, s_buf, m_buf, o_all):
-    both = (mine_ref, other_ref)
-    for i, ref in enumerate(both):
-        for place in range(PLACES):
-            cols = slice((i * PLACES + place) * TOK, (i * PLACES + place + 1) * TOK)
-            v_all[0, :HALF, cols] = ref[place, :TOK].T[HALF:]
-            v_all[1, :HALF, cols] = ref[place, KV_TWO:Q_TWO].T[HALF:]
-    v_all[:, HALF:] = jnp.ones((2, V_ROWS - HALF, KEYS), BF)
+def lay_values(ref, v_all):
+    for place in range(PLACES):
+        cols = slice(place * TOK, (place + 1) * TOK)
+        v_all[0, :HALF, cols] = ref[place, :TOK].T[HALF:]
+        v_all[1, :HALF, cols] = ref[place, KV_TWO:Q_TWO].T[HALF:]
+    v_all[:, HALF:] = jnp.ones((2, V_ROWS - HALF, KEYS // 2), BF)
+
+
+def lay_mine_kernel(mine_ref, v_all, q_all):
+    lay_values(mine_ref, v_all)
 
     def unfold(q, at):
         n = q.shape[0]
@@ -120,10 +122,15 @@
         q_all[at : at + n] = jnp.where(low, q, nil)
         q_all[at + n : at + 2 * n] = jnp.where(low, half_turn(q), nil)
 
-    first = PLACES * TOK
     for place in range(PLACES):
         unfold(mine_ref[place, Q_ONE:KV_TWO], place * TOK)
-        unfold(mine_ref[place, Q_TWO:], first + place * HALF)
+        unfold(mine_ref[place, Q_TWO:], PLACES * TOK + place * HALF)
+
+
+def self_kernel(mine_ref, other_ref, v_mine, q_all, o_ref, v_other, s_buf, m_buf, o_all):
+    both, v_both = (mine_ref, other_ref), (v_mine, v_other)
+    lay_values(other_ref, v_other)
+    first = PLACES * TOK
     change = first // BQ
     steps = change + change // 2
 
@@ -145,9 +152,9 @@
         for t in range(KEYS // KT):
             s = s_buf[slot, t * KT : (t + 1) * KT]
             w = jnp.exp2(s * SCALE - top).astype(BF)
-            total = total + jnp.dot(
-                v_all[i // change, :, t * KT : (t + 1) * KT], w, preferred_element_type=F32
-            )
+            half, at = divmod(t * KT, KEYS // 2)
+            vals = v_both[half][i // change, :, at : at + KT]
+            total = total + jnp.dot(vals, w, preferred_element_type=F32)
         out = total[:HALF] / total[HALF : HALF + 1]
         out = jnp.concatenate([out, out], axis=0).T
         o_all[pl.ds(pl.multiple_of(i * BQ, BQ), BQ)] = out
@@ -201,16 +208,18 @@
 
 def layout_kernel(*refs):
     in_refs, far_ref, o_refs = refs[:NY], refs[NY], refs[NY + 1 : 2 * NY + 1]
-    kv_all, uses_vec, uses_ref = refs[2 * NY + 1 :]
+    kv_all, uses_vec, uses_ref, sem = refs[2 * NY + 1 :]
     cam = lax.axis_index("cam")
     x_hi, y = cam // NY, lax.rem(cam, NY)
     for d in range(NY):
         uses_vec[d : d + 1] = in_refs[d][C_META:, :LANES].astype(F32)[:1].astype(jnp.int32)
     uses_vec[NY:] = jnp.zeros((NY, LANES), jnp.int32)
-    pltpu.sync_copy(uses_vec, uses_ref)
+    copy = pltpu.make_async_copy(uses_vec, uses_ref, sem)
+    copy.start()
     for d in range(NY):
         kv_all[d] = in_refs[d][:C_Q]
         kv_all[NY + d] = far_ref[d * C_Q : (d + 1) * C_Q]
+    copy.wait()
     for d in range(NY):
         places, allowed = [], []
         for j in range(LIST):
@@ -320,12 +329,18 @@
     mine = after(mine, view, to_far, gains)
     other = lax.ppermute(mine, "seq", [(s, s ^ 1) for s in range(4 * NZ)])
     queries = 3 * NZ * TOK
+    v_mine, q_all = pl.pallas_call(
+        lay_mine_kernel,
+        out_shape=[of((2, V_ROWS, KEYS // 2)), of((queries, LANES))],
+        compiler_params=params(),
+        cost_estimate=cost(0, 4 * KEYS * LANES, 0),
+        name="lay_mine",
+    )(mine)
     self_out = pl.pallas_call(
         self_kernel,
         out_shape=of((PLACES, O_ROWS, LANES)),
         scratch_shapes=[
-            pltpu.VMEM((2, V_ROWS, KEYS), BF),
-            pltpu.VMEM((queries, LANES), BF),
+            pltpu.VMEM((2, V_ROWS, KEYS // 2), BF),
             pltpu.VMEM((2, KEYS, BQ), F32),
             pltpu.VMEM((2, 8, BQ), F32),
             pltpu.VMEM((queries, LANES), F32),
@@ -333,7 +348,7 @@
         compiler_params=params(24),
         cost_estimate=cost(16 * queries * KEYS * HALF, 8 * KEYS * LANES, queries * KEYS),
         name="self_attention",
-    )(mine, other)
+    )(mine, other, v_mine, q_all)
     self_back = z_exchange(self_out)
     far = after(far, self_out)
     layout_out = pl.pallas_call(
@@ -343,6 +358,7 @@
             pltpu.VMEM((CAMS, C_Q, GROUP_COLS), BF),
             pltpu.VMEM((CAMS, LANES), jnp.int32),
             pltpu.SMEM((CAMS, LANES), jnp.int32),
+            pltpu.SemaphoreType.DMA(()),
         ],
         compiler_params=params(),
         cost_estimate=cost(16 * TOK * 384 * WIDTH, 4 * TOK * WIDTH, TOK * 384 * 24),

time: 93.1 us -> 92.3 us (level)
  local copies, waits for them, and re-layouts: 1.78 us -> 7.54 us
  starting transfers between devices: 35.5 us -> 33.1 us
  waiting for transfers between devices: 22.6 us -> 20.4 us
  Pallas kernels: 30.4 us -> 28.3 us
    ppermute x1, waiting for transfers between devices: 2.52 us -> 11.1 us  [shards(): lax.ppermute(strip_kv[0, 0], 'cam', [(c, (c - 1) % CAMS) for c in ring])]
    ppermute x1, waiting for transfers between devices: 6.39 us -> 0.01 us  [shards(): lax.ppermute(strip_kv[0, 1], 'cam', [(c, (c + 1) % CAMS) for c in ring])]
    all_to_all x2, waiting for transfers between devices: 5.95 us -> 2.07 us  [z_exchange(): lax.all_to_all(x, 'seq', 0, 0, axis_index_groups=SAME_CORE, tiled=True)]
    unnamed x15 -> x23, local copies, waits for them, and re-layouts: 0.05 us -> 3.03 us
    pallas_call x1, Pallas kernels: 17.8 us -> 15.3 us  [shards(): pl.pallas_call(self_kernel, out_shape=of((PLACES, O_ROWS, LANES)), scratc...]
    ppermute x1, starting transfers between devices: 4.68 us -> 2.17 us  [shards(): lax.ppermute(strip_kv[0, 0], 'cam', [(c, (c - 1) % CAMS) for c in ring])]
    slice x4, local copies, waits for them, and re-layouts: 1.68 us -> 3.79 us  [shards(): to_far = jnp.concatenate([t[:C_Q] for t in got], axis=0)]
    all_to_all x2, starting transfers between devices: 14 us -> 15.2 us  [z_exchange(): lax.all_to_all(x, 'seq', 0, 0, axis_index_groups=SAME_CORE, tiled=True)]
  transfers between devices with their start and end apart: 12 -> 12, of which waited for: 7 -> 5; matrix products, arithmetic and copies ran while one was open for 3% -> 6% of each run, Pallas kernels for 28% -> 27%
where the time goes in v4:
time: 92.3 us; the launch traced here: 91.8 us
  starting transfers between devices  33.1 us (36%)
  Pallas kernels  28.3 us (31%)
  waiting for transfers between devices  20.4 us (22%)
  local copies, waits for them, and re-layouts  7.54 us (8%)
  between operations  1.51 us (2%)
  other arithmetic  0.97 us (1%)
    pallas_call x1, Pallas kernels, shards(): pl.pallas_call(self_kernel, out_shape=of((PLACES, O_ROWS, LANES)), scratc...  15.3 us
    all_to_all x2, starting transfers between devices, z_exchange(): lax.all_to_all(x, 'seq', 0, 0, axis_index_groups=SAME_CORE, tiled=True)  15.2 us
    ppermute x1, waiting for transfers between devices, shards(): lax.ppermute(strip_kv[0, 0], 'cam', [(c, (c - 1) % CAMS) for c in ring])  11.1 us
    ppermute x6, starting transfers between devices, y_send(): return lax.ppermute(x, 'cam', moves)  8.26 us
    ppermute x6, waiting for transfers between devices, y_send(): return lax.ppermute(x, 'cam', moves)  7.27 us
    pallas_call x1, Pallas kernels, shards(): pl.pallas_call(layout_kernel, out_shape=[of((TOK, GROUP_COLS))] * NY, scr...  5.07 us
    ppermute x1, starting transfers between devices, shards(): other = lax.ppermute(mine, 'seq', [(s, s ^ 1) for s in range(4 * NZ)])  5.05 us
    slice x4, local copies, waits for them, and re-layouts, shards(): to_far = jnp.concatenate([t[:C_Q] for t in got], axis=0)  3.79 us
  transfers between devices with their start and end apart: 12, of which 5 were waited for; matrix products, arithmetic and copies ran while one was open for 6% of the time, Pallas kernels for 27%

profile of v4, /device:TPU:1, one launch (start us, length us, event | category | flops | bytes accessed | tf_op | source)
XLA Modules:
  0.0 91.8 jit_solution(14061936370020960591)
XLA Ops:
  0.0 1.7 %pack_z.1 = bf16[16,352,128]{2,1,0:T(8,128)(2,1)S(1)} custom-call(bf16[128,1536]{1,0:T(8,128)(2,1)} %bitcast.15, bf16[128,1536]{1,0:T(8,128)(2,1)} %bitcast.19, bf16[128,1536]{1,0:T(8,128)(2,1)} %bitcast.20), custom_call_target="tpu_custom_call" | custom-call | bytes 2359296 | tf_op jit(solution)/shard_map/pack_z/pallas_call | solution.py:298
  1.7 1.1 %copy-done.1 = bf16[16,352,128]{2,1,0:T(8,128)(2,1)} copy-done((bf16[16,352,128]{2,1,0:T(8,128)(2,1)}, bf16[16,352,128]{2,1,0:T(8,128)(2,1)S(1)}, u32[]{:S(2)}) %copy-start.1) | copy-done | bytes 1441816
  2.9 10.2 %all-to-all-start = ((bf16[16,352,128]{2,1,0:T(8,128)(2,1)}), bf16[16,352,128]{2,1,0:T(8,128)(2,1)S(1)}, u32[]{:S(2)}, u32[]{:S(2)}) async-start(bf16[16,352,128]{2,1,0:T(8,128)(2,1)} %copy-done.1), calls=%async_computation | async-start | bytes 2883584 | tf_op jit(solution)/shard_map/all_to_all | solution.py:283
  13.7 1.0 %copy-done.6 = bf16[128,1536]{1,0:T(8,128)(2,1)S(1)} copy-done((bf16[128,1536]{1,0:T(8,128)(2,1)S(1)}, bf16[128,1536]{1,0:T(8,128)(2,1)}, u32[]{:S(2)}) %copy-start.6) | copy-done | bytes 393240
  14.7 1.6 %pack_cam.1 = (bf16[400,384]{1,0:T(8,128)(2,1)S(1)}, bf16[400,384]{1,0:T(8,128)(2,1)}, bf16[400,384]{1,0:T(8,128)(2,1)}, bf16[400,384]{1,0:T(8,128)(2,1)}) custom-call(s32[1,1,3]{2,1,0:T(1,128)S(1)} %copy-done.9, s32[1,1]{1,0:T(1,128)S(6)} %copy.14.count_ref, bf16[128,1536]{1,0:T(8,128)(2,1)S(1)} %bitcast.16, bf16[128,1536]{1,0:T(8,128)(2,1)S(1)} %copy-done.5, ...), custom_call_target="tpu_custom_call" | custom-call | bytes 2359296 | tf_op jit(solution)/shard_map/pack_cam/pallas_call | solution.py:308
  16.3 1.3 %collective-permute-start.2 = (bf16[400,384]{1,0:T(8,128)(2,1)}, bf16[400,384]{1,0:T(8,128)(2,1)}, u32[]{:S(2)}, u32[]{:S(2)}) collective-permute-start(bf16[400,384]{1,0:T(8,128)(2,1)} %get-tuple-element.18), channel_id=1, source_target_pairs={{0,32},{32,64},{64,96},{96,0},{128,160},{160,192},{192,224},{224,1... | collective-permute-start | bytes 921608 | tf_op jit(solution)/shard_map/ppermute | solution.py:288
  17.6 2.6 %collective-permute-start.3 = (bf16[400,384]{1,0:T(8,128)(2,1)}, bf16[400,384]{1,0:T(8,128)(2,1)}, u32[]{:S(2)}, u32[]{:S(2)}) collective-permute-start(bf16[400,384]{1,0:T(8,128)(2,1)} %get-tuple-element.19), channel_id=1, source_target_pairs={{0,64},{32,96},{64,0},{96,32},{128,192},{160,224},{192,128},{224,1... | collective-permute-start | bytes 921608 | tf_op jit(solution)/shard_map/ppermute | solution.py:288
  20.2 1.1 %collective-permute-start.4 = (bf16[400,384]{1,0:T(8,128)(2,1)}, bf16[400,384]{1,0:T(8,128)(2,1)}, u32[]{:S(2)}, u32[]{:S(2)}) collective-permute-start(bf16[400,384]{1,0:T(8,128)(2,1)} %get-tuple-element.20), channel_id=1, source_target_pairs={{0,96},{32,0},{64,32},{96,64},{128,224},{160,128},{192,160},{224,1... | collective-permute-start | bytes 921608 | tf_op jit(solution)/shard_map/ppermute | solution.py:288
  22.0 2.2 %collective-permute-start.1 = (bf16[2,32,1536]{2,1,0:T(8,128)(2,1)}, bf16[2,32,1536]{2,1,0:T(8,128)(2,1)S(1)}, u32[]{:S(2)}, u32[]{:S(2)}) collective-permute-start(bf16[2,32,1536]{2,1,0:T(8,128)(2,1)} %get-tuple-element.29), channel_id=1, source_target_pairs={{0,224},{32,0},{64,32},{96,64},{128,96},{160,128},{192,160},{224,1... | collective-permute-start | bytes 589832 | tf_op jit(solution)/shard_map/ppermute | solution.py:319
  24.9 0.9 %slice.20 = bf16[256,384]{1,0:T(8,128)(2,1)S(1)} slice(bf16[400,384]{1,0:T(8,128)(2,1)} %copy-done.7), slice={[0:256], [0:384]} | slice | bytes 393216 | tf_op jit(solution)/shard_map/slice | solution.py:327
  25.8 11.1 %collective-permute-done.1.right_ref = bf16[2,32,1536]{2,1,0:T(8,128)(2,1)S(1)} collective-permute-done((bf16[2,32,1536]{2,1,0:T(8,128)(2,1)}, bf16[2,32,1536]{2,1,0:T(8,128)(2,1)S(1)}, u32[]{:S(2)}, u32[]{:S(2)}) %collective-permute-start.1) | collective-permute-done | bytes 196640 | tf_op jit(solution)/shard_map/ppermute | solution.py:319
  36.9 2.1 %view_attention.1.refs_4_ = f32[128,1536]{1,0:T(8,128)S(1)} custom-call(bf16[128,1536]{1,0:T(8,128)(2,1)S(1)} %bitcast.17, bf16[2,32,1536]{2,1,0:T(8,128)(2,1)S(1)} %collective-permute-done.left_ref, bf16[2,32,1536]{2,1,0:T(8,128)(2,1)S(1)} %collective-permute-done.1.right_ref), custom_call_target="tpu_custom_call" | custom-call | flops 201326592 | bytes 786432 | tf_op jit(solution)/shard_map/view_attention/pallas_call | solution.py:320
  42.8 1.0 %pad_maximum_fusion = bf16[1024,384]{1,0:T(8,128)(2,1)} fusion(bf16[256,384]{1,0:T(8,128)(2,1)S(1)} %slice.26, bf16[256,384]{1,0:T(8,128)(2,1)S(1)} %slice.25, bf16[256,384]{1,0:T(8,128)(2,1)S(1)} %slice.24, bf16[256,384]{1,0:T(8,128)(2,1)S(1)} %slice.20), kind=kLoop, calls=%fused_computation | loop fusion | flops 3145728 | bytes 1572864 | tf_op jit(solution)/shard_map/concatenate | solution.py:327
  43.8 2.1 %all-to-all-done.mine_ref = bf16[16,352,128]{2,1,0:T(8,128)(2,1)S(1)} async-done(((bf16[16,352,128]{2,1,0:T(8,128)(2,1)}), bf16[16,352,128]{2,1,0:T(8,128)(2,1)S(1)}, u32[]{:S(2)}, u32[]{:S(2)}) %all-to-all-start) | async-done | bytes 1441824 | tf_op jit(solution)/shard_map/all_to_all | solution.py:283
  45.8 5.1 %collective-permute-start.5 = (bf16[16,352,128]{2,1,0:T(8,128)(2,1)S(1)}, bf16[16,352,128]{2,1,0:T(8,128)(2,1)S(1)}, u32[]{:S(2)}, u32[]{:S(2)}) collective-permute-start(bf16[16,352,128]{2,1,0:T(8,128)(2,1)S(1)} %all-to-all-done.mine_ref), channel_id=1, source_target_pairs={{0,1},{1,0},{2,3},{3,2},{4,5},{5,4},{6,7},{7,6},{8,9},{9,8},{10,11... | collective-permute-start | bytes 4325384 | tf_op jit(solution)/shard_map/ppermute | solution.py:330
  50.9 2.5 %collective-permute-start.6 = (bf16[1024,384]{1,0:T(8,128)(2,1)}, bf16[1024,384]{1,0:T(8,128)(2,1)}, u32[]{:S(2)}, u32[]{:S(2)}) collective-permute-start(bf16[1024,384]{1,0:T(8,128)(2,1)} %pad_maximum_fusion), channel_id=1, source_target_pairs={{0,128},{32,160},{64,192},{96,224},{128,0},{160,32},{192,64},{224,... | collective-permute-start | bytes 2359304 | tf_op jit(solution)/shard_map/ppermute | solution.py:328
  53.8 15.3 %self_attention.1 = bf16[16,96,128]{2,1,0:T(8,128)(2,1)} custom-call(bf16[16,352,128]{2,1,0:T(8,128)(2,1)S(1)} %all-to-all-done.mine_ref, bf16[16,352,128]{2,1,0:T(8,128)(2,1)S(1)} %collective-permute-done.5.other_ref, bf16[2,80,2048]{2,1,0:T(8,128)(2,1)S(1)} %get-tuple-element.22.v_mine, bf16[3072,128]{1,0:T(8,128)(2,1)S(1)} %get-tuple-element.23.q_all), custom_call_target="tpu_custom_call" | custom-call | flops 12884901888 | bytes 4194304 | tf_op jit(solution)/shard_map/self_attention/pallas_call | solution.py:339
  69.1 5.0 %all-to-all-start.1 = ((bf16[16,96,128]{2,1,0:T(8,128)(2,1)}), bf16[16,96,128]{2,1,0:T(8,128)(2,1)}, u32[]{:S(2)}, u32[]{:S(2)}) async-start(bf16[16,96,128]{2,1,0:T(8,128)(2,1)} %self_attention.1), calls=%async_computation.1 | async-start | bytes 786432 | tf_op jit(solution)/shard_map/all_to_all | solution.py:283
  74.1 5.1 %layout_attention.1 = (bf16[128,384]{1,0:T(8,128)(2,1)S(1)}, bf16[128,384]{1,0:T(8,128)(2,1)S(1)}, bf16[128,384]{1,0:T(8,128)(2,1)S(1)}, bf16[128,384]{1,0:T(8,128)(2,1)S(1)}) custom-call(bf16[400,384]{1,0:T(8,128)(2,1)S(1)} %copy-done.8, bf16[400,384]{1,0:T(8,128)(2,1)} %collective-permute-done.2.refs_1_, bf16[400,384]{1,0:T(8,128)(2,1)} %collective-permute-done.3.refs_2_, ...), custom_call_target="tpu_custom_call" | custom-call | flops 1207959552 | bytes 786432 | tf_op jit(solution)/shard_map/layout_attention/pallas_call | solution.py:354
  79.2 2.2 %collective-permute-start.7 = (bf16[128,384]{1,0:T(8,128)(2,1)S(1)}, bf16[128,384]{1,0:T(8,128)(2,1)S(1)}, u32[]{:S(2)}, u32[]{:S(2)}) collective-permute-start(bf16[128,384]{1,0:T(8,128)(2,1)S(1)} %get-tuple-element.26), channel_id=1, source_target_pairs={{0,96},{32,0},{64,32},{96,64},{128,224},{160,128},{192,160},{224,1... | collective-permute-start | bytes 294920 | tf_op jit(solution)/shard_map/ppermute | solution.py:288
  82.5 1.1 %collective-permute-done.7.refs_1_ = bf16[128,384]{1,0:T(8,128)(2,1)S(1)} collective-permute-done((bf16[128,384]{1,0:T(8,128)(2,1)S(1)}, bf16[128,384]{1,0:T(8,128)(2,1)S(1)}, u32[]{:S(2)}, u32[]{:S(2)}) %collective-permute-start.7) | collective-permute-done | bytes 98336 | tf_op jit(solution)/shard_map/ppermute | solution.py:288
  83.6 3.3 %collective-permute-done.8.refs_2_ = bf16[128,384]{1,0:T(8,128)(2,1)S(1)} collective-permute-done((bf16[128,384]{1,0:T(8,128)(2,1)S(1)}, bf16[128,384]{1,0:T(8,128)(2,1)S(1)}, u32[]{:S(2)}, u32[]{:S(2)}) %collective-permute-start.8) | collective-permute-done | bytes 98336 | tf_op jit(solution)/shard_map/ppermute | solution.py:288
  86.8 2.9 %collective-permute-done.9.refs_3_ = bf16[128,384]{1,0:T(8,128)(2,1)S(1)} collective-permute-done((bf16[128,384]{1,0:T(8,128)(2,1)S(1)}, bf16[128,384]{1,0:T(8,128)(2,1)S(1)}, u32[]{:S(2)}, u32[]{:S(2)}) %collective-permute-start.9) | collective-permute-done | bytes 98336 | tf_op jit(solution)/shard_map/ppermute | solution.py:288
  89.7 2.1 %blend.1 = bf16[128,1536]{1,0:T(8,128)(2,1)} custom-call(bf16[16,96,128]{2,1,0:T(8,128)(2,1)} %all-to-all-done.1.self_ref, bf16[128,384]{1,0:T(8,128)(2,1)S(1)} %get-tuple-element.25.refs_0_, bf16[128,384]{1,0:T(8,128)(2,1)S(1)} %collective-permute-done.7.refs_1_, bf16[128,384]{1,0:T(8,128)(2,1)S(1)} %collective-permute-done.8.refs_2_, ...), custom_call_target="tpu_custom_call" | custom-call | bytes 1966080 | tf_op jit(solution)/shard_map/blend/pallas_call | solution.py:368
  (37 shorter events, 6.0 us)
Async XLA Ops:
  0.0 24.8 %copy-start = (f32[50,3,1536]{2,0,1:T(8,128)S(1)}, f32[50,3,1536]{2,0,1:T(8,128)}, u32[]{:S(2)}) copy-start(f32[50,3,1536]{2,0,1:T(8,128)} %param.18) | copy-start | bytes 2764804
  1.7 1.1 %copy-start.1 = (bf16[16,352,128]{2,1,0:T(8,128)(2,1)}, bf16[16,352,128]{2,1,0:T(8,128)(2,1)S(1)}, u32[]{:S(2)}) copy-start(bf16[16,352,128]{2,1,0:T(8,128)(2,1)S(1)} %pack_z.1) | copy-start | bytes 4325380
  2.9 10.8 %copy-start.2 = (bf16[1,128,1536]{2,1,0:T(8,128)(2,1)S(1)}, bf16[1,128,1536]{2,1,0:T(8,128)(2,1)}, u32[]{:S(2)}) copy-start(bf16[1,128,1536]{2,1,0:T(8,128)(2,1)} %param.10) | copy-start | bytes 1179652
  2.9 10.8 %copy-start.5 = (bf16[128,1536]{1,0:T(8,128)(2,1)S(1)}, bf16[128,1536]{1,0:T(8,128)(2,1)}, u32[]{:S(2)}) copy-start(bf16[128,1536]{1,0:T(8,128)(2,1)} %k_ref.1) | copy-start | bytes 1179652
  2.9 10.9 %copy-start.9 = (s32[1,1,3]{2,1,0:T(1,128)S(1)}, s32[1,1,3]{2,1,0:T(1,128)}, u32[]{:S(2)}) copy-start(s32[1,1,3]{2,1,0:T(1,128)} %list_ref.1) | copy-start | bytes 40
  2.9 43.0 %all-to-all-start = ((bf16[16,352,128]{2,1,0:T(8,128)(2,1)}), bf16[16,352,128]{2,1,0:T(8,128)(2,1)S(1)}, u32[]{:S(2)}, u32[]{:S(2)}) async-start(bf16[16,352,128]{2,1,0:T(8,128)(2,1)} %copy-done.1), calls=%async_computation | async-start | bytes 2883584 | tf_op jit(solution)/shard_map/all_to_all | solution.py:283
  13.7 1.0 %copy-start.6 = (bf16[128,1536]{1,0:T(8,128)(2,1)S(1)}, bf16[128,1536]{1,0:T(8,128)(2,1)}, u32[]{:S(2)}) copy-start(bf16[128,1536]{1,0:T(8,128)(2,1)} %v_ref.1) | copy-start | bytes 1179652
  14.7 6.6 %copy-start.10 = (bf16[1,2,2,32,1536]{4,3,2,1,0:T(8,128)(2,1)S(1)}, bf16[1,2,2,32,1536]{4,3,2,1,0:T(8,128)(2,1)}, u32[]{:S(2)}) copy-start(bf16[1,2,2,32,1536]{4,3,2,1,0:T(8,128)(2,1)} %param.13) | copy-start | bytes 1179652
  16.3 7.9 %copy-start.7 = (bf16[400,384]{1,0:T(8,128)(2,1)}, bf16[400,384]{1,0:T(8,128)(2,1)S(1)}, u32[]{:S(2)}) copy-start(bf16[400,384]{1,0:T(8,128)(2,1)S(1)} %get-tuple-element.17.refs_0_) | copy-start | bytes 921604
  16.3 23.6 %collective-permute-start.2 = (bf16[400,384]{1,0:T(8,128)(2,1)}, bf16[400,384]{1,0:T(8,128)(2,1)}, u32[]{:S(2)}, u32[]{:S(2)}) collective-permute-start(bf16[400,384]{1,0:T(8,128)(2,1)} %get-tuple-element.18), channel_id=1, source_target_pairs={{0,32},{32,64},{64,96},{96,0},{128,160},{160,192},{192,224},{224,1... | collective-permute-start | bytes 921608 | tf_op jit(solution)/shard_map/ppermute | solution.py:288
  17.6 23.3 %collective-permute-start.3 = (bf16[400,384]{1,0:T(8,128)(2,1)}, bf16[400,384]{1,0:T(8,128)(2,1)}, u32[]{:S(2)}, u32[]{:S(2)}) collective-permute-start(bf16[400,384]{1,0:T(8,128)(2,1)} %get-tuple-element.19), channel_id=1, source_target_pairs={{0,64},{32,96},{64,0},{96,32},{128,192},{160,224},{192,128},{224,1... | collective-permute-start | bytes 921608 | tf_op jit(solution)/shard_map/ppermute | solution.py:288
  20.2 21.6 %collective-permute-start.4 = (bf16[400,384]{1,0:T(8,128)(2,1)}, bf16[400,384]{1,0:T(8,128)(2,1)}, u32[]{:S(2)}, u32[]{:S(2)}) collective-permute-start(bf16[400,384]{1,0:T(8,128)(2,1)} %get-tuple-element.20), channel_id=1, source_target_pairs={{0,96},{32,0},{64,32},{96,64},{128,224},{160,128},{192,160},{224,1... | collective-permute-start | bytes 921608 | tf_op jit(solution)/shard_map/ppermute | solution.py:288
  22.0 14.9 %collective-permute-start.1 = (bf16[2,32,1536]{2,1,0:T(8,128)(2,1)}, bf16[2,32,1536]{2,1,0:T(8,128)(2,1)S(1)}, u32[]{:S(2)}, u32[]{:S(2)}) collective-permute-start(bf16[2,32,1536]{2,1,0:T(8,128)(2,1)} %get-tuple-element.29), channel_id=1, source_target_pairs={{0,224},{32,0},{64,32},{96,64},{128,96},{160,128},{192,160},{224,1... | collective-permute-start | bytes 589832 | tf_op jit(solution)/shard_map/ppermute | solution.py:319
  24.2 12.7 %collective-permute-start = (bf16[2,32,1536]{2,1,0:T(8,128)(2,1)S(1)}, bf16[2,32,1536]{2,1,0:T(8,128)(2,1)S(1)}, u32[]{:S(2)}, u32[]{:S(2)}) collective-permute-start(bf16[2,32,1536]{2,1,0:T(8,128)(2,1)S(1)} %get-tuple-element.30), channel_id=1, source_target_pairs={{0,32},{32,64},{64,96},{96,128},{128,160},{160,192},{192,224},{224... | collective-permute-start | bytes 589832 | tf_op jit(solution)/shard_map/ppermute | solution.py:318
  39.0 0.9 copy-start.3
  45.8 8.0 %collective-permute-start.5 = (bf16[16,352,128]{2,1,0:T(8,128)(2,1)S(1)}, bf16[16,352,128]{2,1,0:T(8,128)(2,1)S(1)}, u32[]{:S(2)}, u32[]{:S(2)}) collective-permute-start(bf16[16,352,128]{2,1,0:T(8,128)(2,1)S(1)} %all-to-all-done.mine_ref), channel_id=1, source_target_pairs={{0,1},{1,0},{2,3},{3,2},{4,5},{5,4},{6,7},{7,6},{8,9},{9,8},{10,11... | collective-permute-start | bytes 4325384 | tf_op jit(solution)/shard_map/ppermute | solution.py:330
  50.9 23.2 %collective-permute-start.6 = (bf16[1024,384]{1,0:T(8,128)(2,1)}, bf16[1024,384]{1,0:T(8,128)(2,1)}, u32[]{:S(2)}, u32[]{:S(2)}) collective-permute-start(bf16[1024,384]{1,0:T(8,128)(2,1)} %pad_maximum_fusion), channel_id=1, source_target_pairs={{0,128},{32,160},{64,192},{96,224},{128,0},{160,32},{192,64},{224,... | collective-permute-start | bytes 2359304 | tf_op jit(solution)/shard_map/ppermute | solution.py:328
  53.8 20.3 %copy-start.8 = (bf16[400,384]{1,0:T(8,128)(2,1)S(1)}, bf16[400,384]{1,0:T(8,128)(2,1)}, u32[]{:S(2)}) copy-start(bf16[400,384]{1,0:T(8,128)(2,1)} %copy-done.7) | copy-start | bytes 921604
  69.1 20.6 %all-to-all-start.1 = ((bf16[16,96,128]{2,1,0:T(8,128)(2,1)}), bf16[16,96,128]{2,1,0:T(8,128)(2,1)}, u32[]{:S(2)}, u32[]{:S(2)}) async-start(bf16[16,96,128]{2,1,0:T(8,128)(2,1)} %self_attention.1), calls=%async_computation.1 | async-start | bytes 786432 | tf_op jit(solution)/shard_map/all_to_all | solution.py:283
  74.1 15.6 %copy-start.4 = (f32[128,1536]{1,0:T(8,128)S(1)}, f32[128,1536]{1,0:T(8,128)}, u32[]{:S(2)}) copy-start(f32[128,1536]{1,0:T(8,128)} %copy-done.3) | copy-start | bytes 2359300
  79.2 4.4 %collective-permute-start.7 = (bf16[128,384]{1,0:T(8,128)(2,1)S(1)}, bf16[128,384]{1,0:T(8,128)(2,1)S(1)}, u32[]{:S(2)}, u32[]{:S(2)}) collective-permute-start(bf16[128,384]{1,0:T(8,128)(2,1)S(1)} %get-tuple-element.26), channel_id=1, source_target_pairs={{0,96},{32,0},{64,32},{96,64},{128,224},{160,128},{192,160},{224,1... | collective-permute-start | bytes 294920 | tf_op jit(solution)/shard_map/ppermute | solution.py:288
  81.4 5.4 %collective-permute-start.8 = (bf16[128,384]{1,0:T(8,128)(2,1)S(1)}, bf16[128,384]{1,0:T(8,128)(2,1)S(1)}, u32[]{:S(2)}, u32[]{:S(2)}) collective-permute-start(bf16[128,384]{1,0:T(8,128)(2,1)S(1)} %get-tuple-element.27), channel_id=1, source_target_pairs={{0,64},{32,96},{64,0},{96,32},{128,192},{160,224},{192,128},{224,1... | collective-permute-start | bytes 294920 | tf_op jit(solution)/shard_map/ppermute | solution.py:288
  81.8 8.0 %collective-permute-start.9 = (bf16[128,384]{1,0:T(8,128)(2,1)S(1)}, bf16[128,384]{1,0:T(8,128)(2,1)S(1)}, u32[]{:S(2)}, u32[]{:S(2)}) collective-permute-start(bf16[128,384]{1,0:T(8,128)(2,1)S(1)} %get-tuple-element.28), channel_id=1, source_target_pairs={{0,32},{32,64},{64,96},{96,0},{128,160},{160,192},{192,224},{224,1... | collective-permute-start | bytes 294920 | tf_op jit(solution)/shard_map/ppermute | solution.py:288

commit v5 on v4

--- a/solution.py
+++ b/solution.py
@@ -70,14 +70,19 @@
     return pltpu.CompilerParams(vmem_limit_bytes=mib * MIB)
 
 
-def pack_z_kernel(q_hbm, k_hbm, v_hbm, out_ref, q_ref, k_ref, v_ref, sems):
-    pairs = ((k_hbm, k_ref), (v_hbm, v_ref), (q_hbm, q_ref))
-    copies = [pltpu.make_async_copy(a, b, sems.at[i]) for i, (a, b) in enumerate(pairs)]
-    for copy in copies:
-        copy.start()
-    for copy in copies:
-        copy.wait()
+def pack_z_kernel(q_hbm, k_hbm, v_hbm, out_hbm, q_ref, k_ref, v_ref, out_ref, sems, out_sems):
+    half_cols = NZ // 2 * LANES
+    copies = []
+    for part, at in enumerate((2 * half_cols, 0, half_cols)):
+        for i, (a, b) in enumerate(((k_hbm, k_ref), (v_hbm, v_ref), (q_hbm, q_ref))):
+            cols = (slice(None), pl.ds(at, half_cols))
+            copies.append(pltpu.make_async_copy(a.at[cols], b.at[cols], sems.at[part, i]))
+            copies[-1].start()
+    sends = []
     for z in range(NZ):
+        if z % 4 == 0:
+            for copy in copies[:6] if z == 0 else copies[6:]:
+                copy.wait()
         at, half = NZ + z // 2, z % 2
         shared = side_by_side(tile(k_ref, at), half, tile(v_ref, at), half)
         q_shared = tile(q_ref, at)
@@ -88,6 +93,14 @@
             out_ref[place, Q_ONE:KV_TWO] = folded(q, x)
             out_ref[place, KV_TWO:Q_TWO] = shared
             out_ref[place, Q_TWO:] = folded(q_shared[x * HALF : (x + 1) * HALF], half)
+        if z % 4 == 3:
+            done = pl.ds(2 * (z - 3), NZ)
+            sends.append(
+                pltpu.make_async_copy(out_ref.at[done], out_hbm.at[done], out_sems.at[z // 4])
+            )
+            sends[-1].start()
+    for send in sends:
+        send.wait()
 
 
 def pack_cam_kernel(list_ref, count_ref, q_ref, k_ref, v_ref, *outs):
@@ -299,7 +312,10 @@
         pack_z_kernel,
         out_shape=of((PLACES, Z_ROWS, LANES)),
         in_specs=[pl.BlockSpec(memory_space=pltpu.HBM)] * 3,
-        scratch_shapes=[pltpu.VMEM((TOK, WIDTH), BF)] * 3 + [pltpu.SemaphoreType.DMA((3,))],
+        out_specs=pl.BlockSpec(memory_space=pltpu.HBM),
+        scratch_shapes=[pltpu.VMEM((TOK, WIDTH), BF)] * 3
+        + [pltpu.VMEM((PLACES, Z_ROWS, LANES), BF)]
+        + [pltpu.SemaphoreType.DMA((3, 3)), pltpu.SemaphoreType.DMA((2,))],
         compiler_params=params(),
         cost_estimate=cost(0, 2 * 6 * TOK * WIDTH, 0),
         name="pack_z",

time: 92.3 us -> 93 us (level)
  transfers between devices with their start and end apart: 12 -> 12, of which waited for: 5 -> 5; matrix products, arithmetic and copies ran while one was open for 6% -> 6% of each run, Pallas kernels for 27% -> 26%
where the time goes in v5:
time: 93 us; the launch traced here: 92.5 us
  starting transfers between devices  33.1 us (36%)
  Pallas kernels  29 us (31%)
  waiting for transfers between devices  20.4 us (22%)
  local copies, waits for them, and re-layouts  7.54 us (8%)
  between operations  1.51 us (2%)
  other arithmetic  0.97 us (1%)
    pallas_call x1, Pallas kernels, shards(): pl.pallas_call(self_kernel, out_shape=of((PLACES, O_ROWS, LANES)), scratc...  15.2 us
    all_to_all x2, starting transfers between devices, z_exchange(): lax.all_to_all(x, 'seq', 0, 0, axis_index_groups=SAME_CORE, tiled=True)  15.2 us
    ppermute x1, waiting for transfers between devices, shards(): lax.ppermute(strip_kv[0, 0], 'cam', [(c, (c - 1) % CAMS) for c in ring])  11.1 us
    ppermute x6, starting transfers between devices, y_send(): return lax.ppermute(x, 'cam', moves)  8.25 us
    ppermute x6, waiting for transfers between devices, y_send(): return lax.ppermute(x, 'cam', moves)  7.25 us
    pallas_call x1, Pallas kernels, shards(): pl.pallas_call(layout_kernel, out_shape=[of((TOK, GROUP_COLS))] * NY, scr...  5.07 us
    ppermute x1, starting transfers between devices, shards(): other = lax.ppermute(mine, 'seq', [(s, s ^ 1) for s in range(4 * NZ)])  5.05 us
    slice x4, local copies, waits for them, and re-layouts, shards(): to_far = jnp.concatenate([t[:C_Q] for t in got], axis=0)  3.79 us
  transfers between devices with their start and end apart: 12, of which 5 were waited for; matrix products, arithmetic and copies ran while one was open for 6% of the time, Pallas kernels for 26%

profile of v5, /device:TPU:1, one launch (start us, length us, event | category | flops | bytes accessed | tf_op | source)
XLA Modules:
  0.0 92.5 jit_solution(12460015839559195595)
XLA Ops:
  0.0 2.4 %pack_z.1 = bf16[16,352,128]{2,1,0:T(8,128)(2,1)S(1)} custom-call(bf16[128,1536]{1,0:T(8,128)(2,1)} %bitcast.15, bf16[128,1536]{1,0:T(8,128)(2,1)} %bitcast.19, bf16[128,1536]{1,0:T(8,128)(2,1)} %bitcast.20), custom_call_target="tpu_custom_call" | custom-call | bytes 2359296 | tf_op jit(solution)/shard_map/pack_z/pallas_call | solution.py:311
  2.4 1.1 %copy-done.1 = bf16[16,352,128]{2,1,0:T(8,128)(2,1)} copy-done((bf16[16,352,128]{2,1,0:T(8,128)(2,1)}, bf16[16,352,128]{2,1,0:T(8,128)(2,1)S(1)}, u32[]{:S(2)}) %copy-start.1) | copy-done | bytes 1441816
  3.6 10.2 %all-to-all-start = ((bf16[16,352,128]{2,1,0:T(8,128)(2,1)}), bf16[16,352,128]{2,1,0:T(8,128)(2,1)S(1)}, u32[]{:S(2)}, u32[]{:S(2)}) async-start(bf16[16,352,128]{2,1,0:T(8,128)(2,1)} %copy-done.1), calls=%async_computation | async-start | bytes 2883584 | tf_op jit(solution)/shard_map/all_to_all | solution.py:296
  14.4 1.0 %copy-done.6 = bf16[128,1536]{1,0:T(8,128)(2,1)S(1)} copy-done((bf16[128,1536]{1,0:T(8,128)(2,1)S(1)}, bf16[128,1536]{1,0:T(8,128)(2,1)}, u32[]{:S(2)}) %copy-start.6) | copy-done | bytes 393240
  15.4 1.6 %pack_cam.1 = (bf16[400,384]{1,0:T(8,128)(2,1)S(1)}, bf16[400,384]{1,0:T(8,128)(2,1)}, bf16[400,384]{1,0:T(8,128)(2,1)}, bf16[400,384]{1,0:T(8,128)(2,1)}) custom-call(s32[1,1,3]{2,1,0:T(1,128)S(1)} %copy-done.9, s32[1,1]{1,0:T(1,128)S(6)} %copy.14.count_ref, bf16[128,1536]{1,0:T(8,128)(2,1)S(1)} %bitcast.16, bf16[128,1536]{1,0:T(8,128)(2,1)S(1)} %copy-done.5, ...), custom_call_target="tpu_custom_call" | custom-call | bytes 2359296 | tf_op jit(solution)/shard_map/pack_cam/pallas_call | solution.py:324
  17.0 1.3 %collective-permute-start.2 = (bf16[400,384]{1,0:T(8,128)(2,1)}, bf16[400,384]{1,0:T(8,128)(2,1)}, u32[]{:S(2)}, u32[]{:S(2)}) collective-permute-start(bf16[400,384]{1,0:T(8,128)(2,1)} %get-tuple-element.18), channel_id=1, source_target_pairs={{0,32},{32,64},{64,96},{96,0},{128,160},{160,192},{192,224},{224,1... | collective-permute-start | bytes 921608 | tf_op jit(solution)/shard_map/ppermute | solution.py:301
  18.3 2.6 %collective-permute-start.3 = (bf16[400,384]{1,0:T(8,128)(2,1)}, bf16[400,384]{1,0:T(8,128)(2,1)}, u32[]{:S(2)}, u32[]{:S(2)}) collective-permute-start(bf16[400,384]{1,0:T(8,128)(2,1)} %get-tuple-element.19), channel_id=1, source_target_pairs={{0,64},{32,96},{64,0},{96,32},{128,192},{160,224},{192,128},{224,1... | collective-permute-start | bytes 921608 | tf_op jit(solution)/shard_map/ppermute | solution.py:301
  20.9 1.1 %collective-permute-start.4 = (bf16[400,384]{1,0:T(8,128)(2,1)}, bf16[400,384]{1,0:T(8,128)(2,1)}, u32[]{:S(2)}, u32[]{:S(2)}) collective-permute-start(bf16[400,384]{1,0:T(8,128)(2,1)} %get-tuple-element.20), channel_id=1, source_target_pairs={{0,96},{32,0},{64,32},{96,64},{128,224},{160,128},{192,160},{224,1... | collective-permute-start | bytes 921608 | tf_op jit(solution)/shard_map/ppermute | solution.py:301
  22.7 2.2 %collective-permute-start.1 = (bf16[2,32,1536]{2,1,0:T(8,128)(2,1)}, bf16[2,32,1536]{2,1,0:T(8,128)(2,1)S(1)}, u32[]{:S(2)}, u32[]{:S(2)}) collective-permute-start(bf16[2,32,1536]{2,1,0:T(8,128)(2,1)} %get-tuple-element.29), channel_id=1, source_target_pairs={{0,224},{32,0},{64,32},{96,64},{128,96},{160,128},{192,160},{224,1... | collective-permute-start | bytes 589832 | tf_op jit(solution)/shard_map/ppermute | solution.py:335
  25.6 0.9 %slice.20 = bf16[256,384]{1,0:T(8,128)(2,1)S(1)} slice(bf16[400,384]{1,0:T(8,128)(2,1)} %copy-done.7), slice={[0:256], [0:384]} | slice | bytes 393216 | tf_op jit(solution)/shard_map/slice | solution.py:343
  26.5 11.1 %collective-permute-done.1.right_ref = bf16[2,32,1536]{2,1,0:T(8,128)(2,1)S(1)} collective-permute-done((bf16[2,32,1536]{2,1,0:T(8,128)(2,1)}, bf16[2,32,1536]{2,1,0:T(8,128)(2,1)S(1)}, u32[]{:S(2)}, u32[]{:S(2)}) %collective-permute-start.1) | collective-permute-done | bytes 196640 | tf_op jit(solution)/shard_map/ppermute | solution.py:335
  37.6 2.1 %view_attention.1.refs_4_ = f32[128,1536]{1,0:T(8,128)S(1)} custom-call(bf16[128,1536]{1,0:T(8,128)(2,1)S(1)} %bitcast.17, bf16[2,32,1536]{2,1,0:T(8,128)(2,1)S(1)} %collective-permute-done.left_ref, bf16[2,32,1536]{2,1,0:T(8,128)(2,1)S(1)} %collective-permute-done.1.right_ref), custom_call_target="tpu_custom_call" | custom-call | flops 201326592 | bytes 786432 | tf_op jit(solution)/shard_map/view_attention/pallas_call | solution.py:336
  43.5 1.0 %pad_maximum_fusion = bf16[1024,384]{1,0:T(8,128)(2,1)} fusion(bf16[256,384]{1,0:T(8,128)(2,1)S(1)} %slice.26, bf16[256,384]{1,0:T(8,128)(2,1)S(1)} %slice.25, bf16[256,384]{1,0:T(8,128)(2,1)S(1)} %slice.24, bf16[256,384]{1,0:T(8,128)(2,1)S(1)} %slice.20), kind=kLoop, calls=%fused_computation | loop fusion | flops 3145728 | bytes 1572864 | tf_op jit(solution)/shard_map/concatenate | solution.py:343
  44.4 2.1 %all-to-all-done.mine_ref = bf16[16,352,128]{2,1,0:T(8,128)(2,1)S(1)} async-done(((bf16[16,352,128]{2,1,0:T(8,128)(2,1)}), bf16[16,352,128]{2,1,0:T(8,128)(2,1)S(1)}, u32[]{:S(2)}, u32[]{:S(2)}) %all-to-all-start) | async-done | bytes 1441824 | tf_op jit(solution)/shard_map/all_to_all | solution.py:296
  46.5 5.1 %collective-permute-start.5 = (bf16[16,352,128]{2,1,0:T(8,128)(2,1)S(1)}, bf16[16,352,128]{2,1,0:T(8,128)(2,1)S(1)}, u32[]{:S(2)}, u32[]{:S(2)}) collective-permute-start(bf16[16,352,128]{2,1,0:T(8,128)(2,1)S(1)} %all-to-all-done.mine_ref), channel_id=1, source_target_pairs={{0,1},{1,0},{2,3},{3,2},{4,5},{5,4},{6,7},{7,6},{8,9},{9,8},{10,11... | collective-permute-start | bytes 4325384 | tf_op jit(solution)/shard_map/ppermute | solution.py:346
  51.6 2.5 %collective-permute-start.6 = (bf16[1024,384]{1,0:T(8,128)(2,1)}, bf16[1024,384]{1,0:T(8,128)(2,1)}, u32[]{:S(2)}, u32[]{:S(2)}) collective-permute-start(bf16[1024,384]{1,0:T(8,128)(2,1)} %pad_maximum_fusion), channel_id=1, source_target_pairs={{0,128},{32,160},{64,192},{96,224},{128,0},{160,32},{192,64},{224,... | collective-permute-start | bytes 2359304 | tf_op jit(solution)/shard_map/ppermute | solution.py:344
  54.5 15.2 %self_attention.1 = bf16[16,96,128]{2,1,0:T(8,128)(2,1)} custom-call(bf16[16,352,128]{2,1,0:T(8,128)(2,1)S(1)} %all-to-all-done.mine_ref, bf16[16,352,128]{2,1,0:T(8,128)(2,1)S(1)} %collective-permute-done.5.other_ref, bf16[2,80,2048]{2,1,0:T(8,128)(2,1)S(1)} %get-tuple-element.22.v_mine, bf16[3072,128]{1,0:T(8,128)(2,1)S(1)} %get-tuple-element.23.q_all), custom_call_target="tpu_custom_call" | custom-call | flops 12884901888 | bytes 4194304 | tf_op jit(solution)/shard_map/self_attention/pallas_call | solution.py:355
  69.8 5.0 %all-to-all-start.1 = ((bf16[16,96,128]{2,1,0:T(8,128)(2,1)}), bf16[16,96,128]{2,1,0:T(8,128)(2,1)}, u32[]{:S(2)}, u32[]{:S(2)}) async-start(bf16[16,96,128]{2,1,0:T(8,128)(2,1)} %self_attention.1), calls=%async_computation.1 | async-start | bytes 786432 | tf_op jit(solution)/shard_map/all_to_all | solution.py:296
  74.8 5.1 %layout_attention.1 = (bf16[128,384]{1,0:T(8,128)(2,1)S(1)}, bf16[128,384]{1,0:T(8,128)(2,1)S(1)}, bf16[128,384]{1,0:T(8,128)(2,1)S(1)}, bf16[128,384]{1,0:T(8,128)(2,1)S(1)}) custom-call(bf16[400,384]{1,0:T(8,128)(2,1)S(1)} %copy-done.8, bf16[400,384]{1,0:T(8,128)(2,1)} %collective-permute-done.2.refs_1_, bf16[400,384]{1,0:T(8,128)(2,1)} %collective-permute-done.3.refs_2_, ...), custom_call_target="tpu_custom_call" | custom-call | flops 1207959552 | bytes 786432 | tf_op jit(solution)/shard_map/layout_attention/pallas_call | solution.py:370
  79.9 2.2 %collective-permute-start.7 = (bf16[128,384]{1,0:T(8,128)(2,1)S(1)}, bf16[128,384]{1,0:T(8,128)(2,1)S(1)}, u32[]{:S(2)}, u32[]{:S(2)}) collective-permute-start(bf16[128,384]{1,0:T(8,128)(2,1)S(1)} %get-tuple-element.26), channel_id=1, source_target_pairs={{0,96},{32,0},{64,32},{96,64},{128,224},{160,128},{192,160},{224,1... | collective-permute-start | bytes 294920 | tf_op jit(solution)/shard_map/ppermute | solution.py:301
  83.2 1.1 %collective-permute-done.7.refs_1_ = bf16[128,384]{1,0:T(8,128)(2,1)S(1)} collective-permute-done((bf16[128,384]{1,0:T(8,128)(2,1)S(1)}, bf16[128,384]{1,0:T(8,128)(2,1)S(1)}, u32[]{:S(2)}, u32[]{:S(2)}) %collective-permute-start.7) | collective-permute-done | bytes 98336 | tf_op jit(solution)/shard_map/ppermute | solution.py:301
  84.2 3.3 %collective-permute-done.8.refs_2_ = bf16[128,384]{1,0:T(8,128)(2,1)S(1)} collective-permute-done((bf16[128,384]{1,0:T(8,128)(2,1)S(1)}, bf16[128,384]{1,0:T(8,128)(2,1)S(1)}, u32[]{:S(2)}, u32[]{:S(2)}) %collective-permute-start.8) | collective-permute-done | bytes 98336 | tf_op jit(solution)/shard_map/ppermute | solution.py:301
  87.5 2.9 %collective-permute-done.9.refs_3_ = bf16[128,384]{1,0:T(8,128)(2,1)S(1)} collective-permute-done((bf16[128,384]{1,0:T(8,128)(2,1)S(1)}, bf16[128,384]{1,0:T(8,128)(2,1)S(1)}, u32[]{:S(2)}, u32[]{:S(2)}) %collective-permute-start.9) | collective-permute-done | bytes 98336 | tf_op jit(solution)/shard_map/ppermute | solution.py:301
  90.4 2.1 %blend.1 = bf16[128,1536]{1,0:T(8,128)(2,1)} custom-call(bf16[16,96,128]{2,1,0:T(8,128)(2,1)} %all-to-all-done.1.self_ref, bf16[128,384]{1,0:T(8,128)(2,1)S(1)} %get-tuple-element.25.refs_0_, bf16[128,384]{1,0:T(8,128)(2,1)S(1)} %collective-permute-done.7.refs_1_, bf16[128,384]{1,0:T(8,128)(2,1)S(1)} %collective-permute-done.8.refs_2_, ...), custom_call_target="tpu_custom_call" | custom-call | bytes 1966080 | tf_op jit(solution)/shard_map/blend/pallas_call | solution.py:384
  (37 shorter events, 6.0 us)
Async XLA Ops:
  0.0 25.5 %copy-start = (f32[50,3,1536]{2,0,1:T(8,128)S(1)}, f32[50,3,1536]{2,0,1:T(8,128)}, u32[]{:S(2)}) copy-start(f32[50,3,1536]{2,0,1:T(8,128)} %param.18) | copy-start | bytes 2764804
  2.4 1.1 %copy-start.1 = (bf16[16,352,128]{2,1,0:T(8,128)(2,1)}, bf16[16,352,128]{2,1,0:T(8,128)(2,1)S(1)}, u32[]{:S(2)}) copy-start(bf16[16,352,128]{2,1,0:T(8,128)(2,1)S(1)} %pack_z.1) | copy-start | bytes 4325380
  3.6 10.8 %copy-start.2 = (bf16[1,128,1536]{2,1,0:T(8,128)(2,1)S(1)}, bf16[1,128,1536]{2,1,0:T(8,128)(2,1)}, u32[]{:S(2)}) copy-start(bf16[1,128,1536]{2,1,0:T(8,128)(2,1)} %param.10) | copy-start | bytes 1179652
  3.6 10.8 %copy-start.5 = (bf16[128,1536]{1,0:T(8,128)(2,1)S(1)}, bf16[128,1536]{1,0:T(8,128)(2,1)}, u32[]{:S(2)}) copy-start(bf16[128,1536]{1,0:T(8,128)(2,1)} %k_ref.1) | copy-start | bytes 1179652
  3.6 10.9 %copy-start.9 = (s32[1,1,3]{2,1,0:T(1,128)S(1)}, s32[1,1,3]{2,1,0:T(1,128)}, u32[]{:S(2)}) copy-start(s32[1,1,3]{2,1,0:T(1,128)} %list_ref.1) | copy-start | bytes 40
  3.6 43.0 %all-to-all-start = ((bf16[16,352,128]{2,1,0:T(8,128)(2,1)}), bf16[16,352,128]{2,1,0:T(8,128)(2,1)S(1)}, u32[]{:S(2)}, u32[]{:S(2)}) async-start(bf16[16,352,128]{2,1,0:T(8,128)(2,1)} %copy-done.1), calls=%async_computation | async-start | bytes 2883584 | tf_op jit(solution)/shard_map/all_to_all | solution.py:296
  14.4 1.0 %copy-start.6 = (bf16[128,1536]{1,0:T(8,128)(2,1)S(1)}, bf16[128,1536]{1,0:T(8,128)(2,1)}, u32[]{:S(2)}) copy-start(bf16[128,1536]{1,0:T(8,128)(2,1)} %v_ref.1) | copy-start | bytes 1179652
  15.4 6.6 %copy-start.10 = (bf16[1,2,2,32,1536]{4,3,2,1,0:T(8,128)(2,1)S(1)}, bf16[1,2,2,32,1536]{4,3,2,1,0:T(8,128)(2,1)}, u32[]{:S(2)}) copy-start(bf16[1,2,2,32,1536]{4,3,2,1,0:T(8,128)(2,1)} %param.13) | copy-start | bytes 1179652
  17.0 7.9 %copy-start.7 = (bf16[400,384]{1,0:T(8,128)(2,1)}, bf16[400,384]{1,0:T(8,128)(2,1)S(1)}, u32[]{:S(2)}) copy-start(bf16[400,384]{1,0:T(8,128)(2,1)S(1)} %get-tuple-element.17.refs_0_) | copy-start | bytes 921604
  17.0 23.6 %collective-permute-start.2 = (bf16[400,384]{1,0:T(8,128)(2,1)}, bf16[400,384]{1,0:T(8,128)(2,1)}, u32[]{:S(2)}, u32[]{:S(2)}) collective-permute-start(bf16[400,384]{1,0:T(8,128)(2,1)} %get-tuple-element.18), channel_id=1, source_target_pairs={{0,32},{32,64},{64,96},{96,0},{128,160},{160,192},{192,224},{224,1... | collective-permute-start | bytes 921608 | tf_op jit(solution)/shard_map/ppermute | solution.py:301
  18.3 23.3 %collective-permute-start.3 = (bf16[400,384]{1,0:T(8,128)(2,1)}, bf16[400,384]{1,0:T(8,128)(2,1)}, u32[]{:S(2)}, u32[]{:S(2)}) collective-permute-start(bf16[400,384]{1,0:T(8,128)(2,1)} %get-tuple-element.19), channel_id=1, source_target_pairs={{0,64},{32,96},{64,0},{96,32},{128,192},{160,224},{192,128},{224,1... | collective-permute-start | bytes 921608 | tf_op jit(solution)/shard_map/ppermute | solution.py:301
  20.9 21.6 %collective-permute-start.4 = (bf16[400,384]{1,0:T(8,128)(2,1)}, bf16[400,384]{1,0:T(8,128)(2,1)}, u32[]{:S(2)}, u32[]{:S(2)}) collective-permute-start(bf16[400,384]{1,0:T(8,128)(2,1)} %get-tuple-element.20), channel_id=1, source_target_pairs={{0,96},{32,0},{64,32},{96,64},{128,224},{160,128},{192,160},{224,1... | collective-permute-start | bytes 921608 | tf_op jit(solution)/shard_map/ppermute | solution.py:301
  22.7 14.9 %collective-permute-start.1 = (bf16[2,32,1536]{2,1,0:T(8,128)(2,1)}, bf16[2,32,1536]{2,1,0:T(8,128)(2,1)S(1)}, u32[]{:S(2)}, u32[]{:S(2)}) collective-permute-start(bf16[2,32,1536]{2,1,0:T(8,128)(2,1)} %get-tuple-element.29), channel_id=1, source_target_pairs={{0,224},{32,0},{64,32},{96,64},{128,96},{160,128},{192,160},{224,1... | collective-permute-start | bytes 589832 | tf_op jit(solution)/shard_map/ppermute | solution.py:335
  24.9 12.7 %collective-permute-start = (bf16[2,32,1536]{2,1,0:T(8,128)(2,1)S(1)}, bf16[2,32,1536]{2,1,0:T(8,128)(2,1)S(1)}, u32[]{:S(2)}, u32[]{:S(2)}) collective-permute-start(bf16[2,32,1536]{2,1,0:T(8,128)(2,1)S(1)} %get-tuple-element.30), channel_id=1, source_target_pairs={{0,32},{32,64},{64,96},{96,128},{128,160},{160,192},{192,224},{224... | collective-permute-start | bytes 589832 | tf_op jit(solution)/shard_map/ppermute | solution.py:334
  39.7 0.9 copy-start.3
  46.5 8.0 %collective-permute-start.5 = (bf16[16,352,128]{2,1,0:T(8,128)(2,1)S(1)}, bf16[16,352,128]{2,1,0:T(8,128)(2,1)S(1)}, u32[]{:S(2)}, u32[]{:S(2)}) collective-permute-start(bf16[16,352,128]{2,1,0:T(8,128)(2,1)S(1)} %all-to-all-done.mine_ref), channel_id=1, source_target_pairs={{0,1},{1,0},{2,3},{3,2},{4,5},{5,4},{6,7},{7,6},{8,9},{9,8},{10,11... | collective-permute-start | bytes 4325384 | tf_op jit(solution)/shard_map/ppermute | solution.py:346
  51.6 23.2 %collective-permute-start.6 = (bf16[1024,384]{1,0:T(8,128)(2,1)}, bf16[1024,384]{1,0:T(8,128)(2,1)}, u32[]{:S(2)}, u32[]{:S(2)}) collective-permute-start(bf16[1024,384]{1,0:T(8,128)(2,1)} %pad_maximum_fusion), channel_id=1, source_target_pairs={{0,128},{32,160},{64,192},{96,224},{128,0},{160,32},{192,64},{224,... | collective-permute-start | bytes 2359304 | tf_op jit(solution)/shard_map/ppermute | solution.py:344
  54.5 20.3 %copy-start.8 = (bf16[400,384]{1,0:T(8,128)(2,1)S(1)}, bf16[400,384]{1,0:T(8,128)(2,1)}, u32[]{:S(2)}) copy-start(bf16[400,384]{1,0:T(8,128)(2,1)} %copy-done.7) | copy-start | bytes 921604
  69.8 20.6 %all-to-all-start.1 = ((bf16[16,96,128]{2,1,0:T(8,128)(2,1)}), bf16[16,96,128]{2,1,0:T(8,128)(2,1)}, u32[]{:S(2)}, u32[]{:S(2)}) async-start(bf16[16,96,128]{2,1,0:T(8,128)(2,1)} %self_attention.1), calls=%async_computation.1 | async-start | bytes 786432 | tf_op jit(solution)/shard_map/all_to_all | solution.py:296
  74.8 15.6 %copy-start.4 = (f32[128,1536]{1,0:T(8,128)S(1)}, f32[128,1536]{1,0:T(8,128)}, u32[]{:S(2)}) copy-start(f32[128,1536]{1,0:T(8,128)} %copy-done.3) | copy-start | bytes 2359300
  79.9 4.3 %collective-permute-start.7 = (bf16[128,384]{1,0:T(8,128)(2,1)S(1)}, bf16[128,384]{1,0:T(8,128)(2,1)S(1)}, u32[]{:S(2)}, u32[]{:S(2)}) collective-permute-start(bf16[128,384]{1,0:T(8,128)(2,1)S(1)} %get-tuple-element.26), channel_id=1, source_target_pairs={{0,96},{32,0},{64,32},{96,64},{128,224},{160,128},{192,160},{224,1... | collective-permute-start | bytes 294920 | tf_op jit(solution)/shard_map/ppermute | solution.py:301
  82.1 5.4 %collective-permute-start.8 = (bf16[128,384]{1,0:T(8,128)(2,1)S(1)}, bf16[128,384]{1,0:T(8,128)(2,1)S(1)}, u32[]{:S(2)}, u32[]{:S(2)}) collective-permute-start(bf16[128,384]{1,0:T(8,128)(2,1)S(1)} %get-tuple-element.27), channel_id=1, source_target_pairs={{0,64},{32,96},{64,0},{96,32},{128,192},{160,224},{192,128},{224,1... | collective-permute-start | bytes 294920 | tf_op jit(solution)/shard_map/ppermute | solution.py:301
  82.5 7.9 %collective-permute-start.9 = (bf16[128,384]{1,0:T(8,128)(2,1)S(1)}, bf16[128,384]{1,0:T(8,128)(2,1)S(1)}, u32[]{:S(2)}, u32[]{:S(2)}) collective-permute-start(bf16[128,384]{1,0:T(8,128)(2,1)S(1)} %get-tuple-element.28), channel_id=1, source_target_pairs={{0,32},{32,64},{64,96},{96,0},{128,160},{160,192},{192,224},{224,1... | collective-permute-start | bytes 294920 | tf_op jit(solution)/shard_map/ppermute | solution.py:301
